TPU v7x, 32 devices: a whole 2x2x4 slice. The times are simulated.
32 devices in a mesh: gx: 4 (over z), gy: 8 (over y, x, core).
Axes of the slice: x: 2, y: 2, z: 4, core: 2. Of those that a mesh axis runs over, the one named last changes fastest.
Arguments:
- points: bfloat16 [1, 32768, 256], P(None, ('gx', 'gy')), may hold values from -16 to 16
- send_rows: int32 [1, 32, 768], P(None, ('gx', 'gy')), may hold values from 0 to 1023, as said below
- recv_slot: int32 [1, 32768], P(None, ('gx', 'gy')), may hold values from 0 to 1791, as said below
- norm1_gain: float32 [256], replicated, may hold values from 0.1 to 1.9
- qkv_weight: bfloat16 [256, 768], replicated, may hold values from -0.375 to 0.375
- proj_weight: bfloat16 [256, 256], replicated, may hold values from -0.375 to 0.375
- norm2_gain: float32 [256], replicated, may hold values from 0.1 to 1.9
- fc1_weight: bfloat16 [256, 1024], replicated, may hold values from -0.375 to 0.375
- fc2_weight: bfloat16 [1024, 256], replicated, may hold values from -0.1875 to 0.1875
- cotangent: bfloat16 [1, 32768, 256], P(None, ('gx', 'gy')), may hold values from -6 to 6
Outputs:
- block_out: bfloat16 [1, 32768, 256], P(None, ('gx', 'gy'))
- grad_points: bfloat16 [1, 32768, 256], P(None, ('gx', 'gy'))
Inputs may be any that keep to these rules, and one draw needn't show every extreme that they name: `send_rows`: for every event and source device a, the first L(a) of the slots toward a - 1 and the first R(a) of the slots toward a + 1 (devices mod 32) are used; the rows they name are distinct and, with the rows that recv_slot of device a lists as its own, cover all 1024 rows of a. Unused slots name arbitrary rows. L(a) and R(a) are at most 384, and in every event some device sends exactly 384 points to its next device. `recv_slot`: for every event and destination device d, the 1024 entries of d's block are distinct: a value s < 1024 names d's own z-order row s, 1024 + c the c-th slot of device d - 1 toward d, 1408 + c the c-th slot of device d + 1 toward d (mod 32); exactly the used slots appear, so that the Hilbert order is a permutation of the z-order in which every point moves at most one device along the curve.
All inputs are finite; a program needn't handle non-finite values.
Results may differ from a plain program's by a relative error of at most 0.0054.
Values may be sent and summed in bfloat16 or wider, within the bound.
A program may use at most 128 MiB of HBM per device.

v0:
```python
import math

import jax
import jax.numpy as jnp
from jax import lax
from jax.sharding import PartitionSpec as P

H = 16
K = 1024
SHIFT = 512


epsilon = 1e-05


def with_halo(cells, sides, width):
    for axis, dim in sides:
        count = lax.axis_size(axis)
        head = lax.slice_in_dim(cells, 0, width, axis=dim)
        tail = lax.slice_in_dim(cells, cells.shape[dim] - width, cells.shape[dim], axis=dim)
        cells = jnp.concatenate(
            [
                lax.ppermute(tail, axis, [(i, (i + 1) % count) for i in range(count)]),
                cells,
                lax.ppermute(head, axis, [((i + 1) % count, i) for i in range(count)]),
            ],
            axis=dim,
        )
    return cells


def norm_rows(row_block, gain):
    row_mean = jnp.mean(row_block, axis=-1, keepdims=True)
    centered = row_block - row_mean
    spread = jnp.mean(centered * centered, axis=-1, keepdims=True)
    return centered * lax.rsqrt(spread + epsilon) * gain


def gelu_exact(values):
    return jax.nn.gelu(values, approximate=False)


def front(ordered, norm1_gain, qkv_weight):
    normed = norm_rows(ordered.astype(jnp.float32), norm1_gain).astype(jnp.bfloat16)
    return jnp.dot(normed, qkv_weight, preferred_element_type=jnp.float32).astype(jnp.bfloat16)


def rest_pass(ordered, attention, norm2_gain, proj_weight, fc1_weight, fc2_weight, cotangent):
    mixed_rows = ordered.astype(jnp.float32) + jnp.dot(
        attention, proj_weight, preferred_element_type=jnp.float32
    )
    normed_two, norm_back = jax.vjp(lambda row_block: norm_rows(row_block, norm2_gain), mixed_rows)
    hidden_pre = jnp.dot(
        normed_two.astype(jnp.bfloat16), fc1_weight, preferred_element_type=jnp.float32
    )
    activated, gelu_back = jax.vjp(gelu_exact, hidden_pre)
    activated_b = activated.astype(jnp.bfloat16)
    block_out = (
        mixed_rows + jnp.dot(activated_b, fc2_weight, preferred_element_type=jnp.float32)
    ).astype(jnp.bfloat16)
    grad_act = jnp.dot(cotangent, fc2_weight.T, preferred_element_type=jnp.float32)
    grad_pre = gelu_back(grad_act)[0].astype(jnp.bfloat16)
    grad_normed = jnp.dot(grad_pre, fc1_weight.T, preferred_element_type=jnp.float32)
    grad_mixed = cotangent.astype(jnp.float32) + norm_back(grad_normed)[0]
    grad_attention = jnp.dot(
        grad_mixed.astype(jnp.bfloat16), proj_weight.T, preferred_element_type=jnp.float32
    ).astype(jnp.bfloat16)
    return (block_out, grad_attention, grad_mixed)


def front_backward(ordered, grad_qkv, grad_mixed, norm1_gain, qkv_weight):
    unused, norm_back = jax.vjp(
        lambda row_block: norm_rows(row_block, norm1_gain), ordered.astype(jnp.float32)
    )
    grad_normed = jnp.dot(
        grad_qkv.astype(jnp.bfloat16), qkv_weight.T, preferred_element_type=jnp.float32
    )
    return (grad_mixed + norm_back(grad_normed)[0]).astype(jnp.bfloat16)


def split_heads(matrix, head_count):
    return matrix.reshape(matrix.shape[0], head_count, matrix.shape[1] // head_count)


def attend(queries, key_rows, value_rows, head_count):
    row_count = queries.shape[0]
    head_size = queries.shape[1] // head_count
    score_scale = 1.0 / math.sqrt(head_size)
    query_heads = split_heads(queries, head_count)
    key_heads = split_heads(key_rows, head_count)
    value_heads = split_heads(value_rows, head_count)
    scores = (
        jnp.einsum("qhd,khd->hqk", query_heads, key_heads, preferred_element_type=jnp.float32)
        * score_scale
    )
    weights = jnp.exp(scores)
    probs_b = (weights / jnp.sum(weights, axis=-1, keepdims=True)).astype(jnp.bfloat16)
    result = jnp.einsum("hqk,khd->qhd", probs_b, value_heads, preferred_element_type=jnp.float32)
    return result.reshape(row_count, -1).astype(jnp.bfloat16)


def attend_backward(queries, key_rows, value_rows, grad_out, head_count):
    row_count = queries.shape[0]
    window = key_rows.shape[0]
    head_size = queries.shape[1] // head_count
    score_scale = 1.0 / math.sqrt(head_size)
    query_heads = split_heads(queries, head_count)
    key_heads = split_heads(key_rows, head_count)
    value_heads = split_heads(value_rows, head_count)
    grad_heads = split_heads(grad_out, head_count)
    scores = (
        jnp.einsum("qhd,khd->hqk", query_heads, key_heads, preferred_element_type=jnp.float32)
        * score_scale
    )
    weights = jnp.exp(scores)
    probs_full = weights / jnp.sum(weights, axis=-1, keepdims=True)
    probs_b = probs_full.astype(jnp.bfloat16)
    grad_probs = jnp.einsum(
        "qhd,khd->hqk", grad_heads, value_heads, preferred_element_type=jnp.float32
    )
    grad_values = jnp.einsum(
        "hqk,qhd->khd", probs_b, grad_heads, preferred_element_type=jnp.float32
    )
    inner_sum = jnp.sum(probs_full * grad_probs, axis=-1, keepdims=True)
    grad_scores = (probs_full * (grad_probs - inner_sum) * score_scale).astype(jnp.bfloat16)
    grad_queries = jnp.einsum(
        "hqk,khd->qhd", grad_scores, key_heads, preferred_element_type=jnp.float32
    )
    grad_keys = jnp.einsum(
        "hqk,qhd->khd", grad_scores, query_heads, preferred_element_type=jnp.float32
    )
    return (
        grad_queries.reshape(row_count, -1),
        grad_keys.reshape(window, -1),
        grad_values.reshape(window, -1),
    )


def shards(
    points,
    send_rows,
    recv_slot,
    norm1_gain,
    qkv_weight,
    proj_weight,
    norm2_gain,
    fc1_weight,
    fc2_weight,
    cotangent,
):
    event_count, row_count, width = points.shape
    slot_count = send_rows.shape[2] // 2
    head_width = proj_weight.shape[0]
    block_count = 2 * row_count // K
    group_heads = math.gcd(H, 4)
    group_count = H // group_heads
    group_width = group_heads * (head_width // H)
    local_points = points[0]
    sender = send_rows[0, 0]
    outgoing = local_points[sender]
    arrived = with_halo(outgoing, ((("gx", "gy"), 0),), slot_count)
    pool = jnp.concatenate([local_points, arrived[:slot_count], arrived[-slot_count:]], axis=0)
    slot_index = recv_slot[0]
    ordered = pool[slot_index]
    qkv = front(ordered, norm1_gain, qkv_weight)
    queries = qkv[:, :head_width]
    key_values = qkv[:, head_width:]
    extended = with_halo(key_values, ((("gx", "gy"), 0),), SHIFT)

    def forward_block(block_index):
        query_rows = lax.dynamic_slice_in_dim(queries, block_index * SHIFT, SHIFT, 0)
        window_rows = lax.dynamic_slice_in_dim(extended, (block_index + 1) // 2 * K, K, 0)
        return attend(query_rows, window_rows[:, :head_width], window_rows[:, head_width:], H)

    block_ids = jnp.arange(block_count, dtype=jnp.int32)
    attention = lax.map(forward_block, block_ids).reshape(row_count, head_width)
    block_out, grad_attention, grad_mixed = rest_pass(
        ordered, attention, norm2_gain, proj_weight, fc1_weight, fc2_weight, cotangent[0]
    )

    def backward_block(block_index):
        query_rows = lax.dynamic_slice_in_dim(queries, block_index * SHIFT, SHIFT, 0)
        grad_rows = lax.dynamic_slice_in_dim(grad_attention, block_index * SHIFT, SHIFT, 0)
        window_rows = lax.dynamic_slice_in_dim(extended, (block_index + 1) // 2 * K, K, 0)
        key_rows = window_rows[:, :head_width]
        value_rows = window_rows[:, head_width:]

        def one_group(group_index):
            start = group_index * group_width

            def columns(matrix):
                return lax.dynamic_slice_in_dim(matrix, start, group_width, 1)

            return attend_backward(
                columns(query_rows),
                columns(key_rows),
                columns(value_rows),
                columns(grad_rows),
                group_heads,
            )

        group_q, group_k, group_v = lax.map(one_group, jnp.arange(group_count, dtype=jnp.int32))
        grad_q = jnp.transpose(group_q, (1, 0, 2)).reshape(SHIFT, head_width)
        grad_k = jnp.transpose(group_k, (1, 0, 2)).reshape(K, head_width)
        grad_v = jnp.transpose(group_v, (1, 0, 2)).reshape(K, head_width)
        return (grad_q, jnp.concatenate([grad_k, grad_v], axis=1))

    grad_q_blocks, grad_windows = lax.map(backward_block, block_ids)
    grad_queries = grad_q_blocks.reshape(row_count, head_width)
    zero_block = jnp.zeros((1, K, 2 * head_width), jnp.float32)
    paired = jnp.concatenate([zero_block, grad_windows, zero_block], axis=0)
    paired = paired.reshape(block_count // 2 + 1, 2, K, 2 * head_width).sum(axis=1)
    paired = paired.reshape((block_count // 2 + 1) * K, 2 * head_width)
    outgoing_grads = jnp.concatenate([paired[:SHIFT], paired[-SHIFT:]], axis=0)
    returned = with_halo(outgoing_grads.astype(jnp.bfloat16), ((("gx", "gy"), 0),), SHIFT).astype(
        outgoing_grads.dtype
    )
    grad_kv = paired[SHIFT : SHIFT + row_count]
    grad_kv = grad_kv.at[:SHIFT].add(returned[:SHIFT])
    grad_kv = grad_kv.at[row_count - SHIFT :].add(returned[-SHIFT:])
    grad_qkv = jnp.concatenate([grad_queries, grad_kv], axis=1)
    grad_ordered = front_backward(ordered, grad_qkv, grad_mixed, norm1_gain, qkv_weight)
    back_pool = (
        jnp.zeros((row_count + 2 * slot_count, width), jnp.bfloat16)
        .at[slot_index]
        .set(grad_ordered)
    )
    back_out = back_pool[row_count:]
    came_back = with_halo(back_out, ((("gx", "gy"), 0),), slot_count)
    returned_rows = jnp.concatenate([came_back[:slot_count], came_back[-slot_count:]], axis=0)
    grad_event = back_pool[:row_count].at[sender].add(returned_rows)
    outputs_list = [block_out]
    grads_list = [grad_event]
    return (jnp.stack(outputs_list), jnp.stack(grads_list))


def solution(mesh):
    in_specs = (
        P(None, ("gx", "gy"), None),
        P(None, ("gx", "gy"), None),
        P(None, ("gx", "gy")),
        P(),
        P(),
        P(),
        P(),
        P(),
        P(),
        P(None, ("gx", "gy"), None),
    )
    out_specs = (P(None, ("gx", "gy"), None), P(None, ("gx", "gy"), None))
    return jax.shard_map(shards, mesh=mesh, in_specs=in_specs, out_specs=out_specs, check_vma=False)
```

profile of v0, /device:TPU:0, one launch (start us, length us, event | category | flops | bytes accessed | tf_op | source)
XLA Modules:
  0.0 661.7 jit_solution(6064685111645509026)
XLA Ops:
  5.3 6.4 collective-permute-start.1
  14.9 5.5 collective-permute-done
  34.4 5.5 collective-permute-done.2
  45.8 63.4 %while.57 = (s32[]{:T(128)}, bf16[2,512,256]{2,1,0:T(8,128)(2,1)}, s32[2]{0:T(128)S(1)}, bf16[2048,512]{0,1:T(8,128)(2,1)S(1)}, bf16[1024,256]{0,1:T(8,128)(2,1)...) while((s32[]{:T(128)}, bf16[2,512,256]{2,1,0:T(8,128)(2,1)}, ...), condition=%wide.region_4.5_spmd, body=%wide.region_2.4_spmd.sunk | while | flops 578936832 | bytes 72417712 | solution.py:176
  49.6 13.6 %fusion.141 = (f32[16,512]{1,0:T(8,128)S(1)}, f32[16,512,1024]{2,1,0:T(8,128)}) fusion(bf16[512,16,16]{0,2,1:T(8,128)(2,1)S(1)} %bitcast.153, bf16[1024,16,16]{0,2,1:T(8,128)(2,1)S(1)} %bitcast.152), kind=kOutput, calls=%fused_computation.6.clone.1 | convolution fusion | flops 285204480 | bytes 34373632 | tf_op jit(solution)/shard_map/while/body/eval_jaxpr/qhd,khd->hqk/dot_general | solution.py:93
  63.3 13.4 %fusion.142 = bf16[16,16,512]{2,1,0:T(8,128)(2,1)S(1)} fusion(bf16[1024,16,16]{0,2,1:T(8,128)(2,1)} %bitcast.161, f32[16,512,1024]{2,1,0:T(8,128)} %get-tuple-element.507, f32[16,512]{1,0:T(8,128)S(1)} %get-tuple-element.508), kind=kOutput, calls=%fused_computation.8.clone.1 | convolution fusion | flops 293732352 | bytes 34373632 | tf_op jit(solution)/shard_map/while/body/eval_jaxpr/hqk,khd->qhd/dot_general | solution.py:98
  81.4 13.6 %fusion.141 = (f32[16,512]{1,0:T(8,128)S(1)}, f32[16,512,1024]{2,1,0:T(8,128)}) fusion(bf16[512,16,16]{0,2,1:T(8,128)(2,1)S(1)} %bitcast.153, bf16[1024,16,16]{0,2,1:T(8,128)(2,1)S(1)} %bitcast.152), kind=kOutput, calls=%fused_computation.6.clone.1 | convolution fusion | flops 285204480 | bytes 34373632 | tf_op jit(solution)/shard_map/while/body/eval_jaxpr/qhd,khd->hqk/dot_general | solution.py:93
  95.0 13.4 %fusion.142 = bf16[16,16,512]{2,1,0:T(8,128)(2,1)S(1)} fusion(bf16[1024,16,16]{0,2,1:T(8,128)(2,1)} %bitcast.161, f32[16,512,1024]{2,1,0:T(8,128)} %get-tuple-element.507, f32[16,512]{1,0:T(8,128)S(1)} %get-tuple-element.508), kind=kOutput, calls=%fused_computation.8.clone.1 | convolution fusion | flops 293732352 | bytes 34373632 | tf_op jit(solution)/shard_map/while/body/eval_jaxpr/hqk,khd->qhd/dot_general | solution.py:98
  111.0 10.9 %fusion.28 = (f32[1024,1024]{1,0:T(8,128)}, f32[1024,1024]{1,0:T(8,128)}) fusion(bf16[256,1024]{1,0:T(8,128)(2,1)S(1)} %copy-done, f32[1024,256]{0,1:T(8,128)S(1)} %get-tuple-element.354, f32[256]{0:T(256)S(1)} %copy-done.32, f32[1024]{0:T(1024)S(1)} %fusion.80, f32[1024]{0:T(1024)S(1)} %broadcast_multiply_fusion), kind=kOutput, calls=%fused_computation.44 | convolution fusion | flops 602931200 | bytes 9970688 | tf_op jit(solution)/shard_map/dot_general | solution.py:53
  121.9 7.5 %multiply_reduce_fusion.1 = (f32[1024]{0:T(1024)S(1)}, f32[1024,256]{0,1:T(8,128)}) fusion(f32[1024,256]{0,1:T(8,128)} %copy-done.8, f32[1024]{0:T(1024)S(1)} %broadcast_multiply_fusion, f32[256]{0:T(256)S(1)} %copy-done.32, bf16[256,1024]{1,0:T(8,128)(2,1)S(1)} %copy-done, f32[1024,1024]{1,0:T(8,128)} %get-tuple-element.355, ...), kind=kOutput, calls=%fused_computation.94 | convolution fusion | flops 1089469440 | bytes 12067840 | tf_op jit(solution)/shard_map/dot_general | solution.py:63
  133.4 476.7 %while.59 = (s32[]{:T(128)}, bf16[2,512,256]{2,1,0:T(8,128)(2,1)}, f32[2,1024,512]{1,2,0:T(8,128)}, s32[2]{0:T(128)S(1)}, bf16[1024,256]{0,1:T(8,128)(2,1)}, /*i...) while((s32[]{:T(128)}, bf16[2,512,256]{2,1,0:T(8,128)(2,1)}, ...), condition=%wide.region_14.15_spmd, body=%wide.region_9.0_spmd.sunk | while | flops 384307232 | bytes 87655400 | solution.py:208
  138.8 228.9 %while.60 = (s32[]{:T(128)}, bf16[4,512,64]{1,2,0:T(8,128)(2,1)S(1)}, f32[4,1024,64]{1,2,0:T(8,128)}, f32[4,1024,64]{1,2,0:T(8,128)}, s32[4]{0:T(128)S(1)}, /*in...) while((s32[]{:T(128)}, ...), condition=%wide.region_13.13_spmd, body=%wide.region_10.12_spmd.sunk | while | flops 383782912 | bytes 61964504 | solution.py:202
  142.0 4.5 fusion.155
  146.5 4.7 fusion.156
  151.2 21.2 %fusion.157 = bf16[4,16,512]{2,1,0:T(8,128)(2,1)S(1)} fusion(bf16[1024,4,16]{0,2,1:T(8,128)(2,1)S(1)} %bitcast.144, f32[4,512,1024]{2,1,0:T(8,128)} %fusion.155, f32[4,512,1024]{2,1,0:T(8,128)} %get-tuple-element.531, f32[4,512]{1,0:T(4,128)S(1)} %get-tuple-element.532), kind=kOutput, calls=%fused_computation.23.clone.1 | convolution fusion | flops 85986304 | bytes 16982016 | tf_op jit(solution)/shard_map/while/body/eval_jaxpr/while/body/eval_jaxpr/hqk,khd->qhd/dot_general | solution.py:126
  176.7 18.5 %fusion.159 = f32[4,16,1024]{2,1,0:T(8,128)S(1)} fusion(bf16[512,4,16]{0,2,1:T(8,128)(2,1)S(1)} %bitcast.149, f32[4,512,1024]{2,1,0:T(8,128)} %fusion.155, f32[4,512,1024]{2,1,0:T(8,128)} %get-tuple-element.531, f32[4,512]{1,0:T(4,128)S(1)} %get-tuple-element.532), kind=kOutput, calls=%fused_computation.22.clone.1 | convolution fusion | flops 85986304 | bytes 17113088 | tf_op jit(solution)/shard_map/while/body/eval_jaxpr/while/body/eval_jaxpr/hqk,qhd->khd/dot_general | solution.py:129
  199.3 4.5 fusion.155
  203.8 4.7 fusion.156
  208.4 21.2 %fusion.157 = bf16[4,16,512]{2,1,0:T(8,128)(2,1)S(1)} fusion(bf16[1024,4,16]{0,2,1:T(8,128)(2,1)S(1)} %bitcast.144, f32[4,512,1024]{2,1,0:T(8,128)} %fusion.155, f32[4,512,1024]{2,1,0:T(8,128)} %get-tuple-element.531, f32[4,512]{1,0:T(4,128)S(1)} %get-tuple-element.532), kind=kOutput, calls=%fused_computation.23.clone.1 | convolution fusion | flops 85986304 | bytes 16982016 | tf_op jit(solution)/shard_map/while/body/eval_jaxpr/while/body/eval_jaxpr/hqk,khd->qhd/dot_general | solution.py:126
  233.9 18.5 %fusion.159 = f32[4,16,1024]{2,1,0:T(8,128)S(1)} fusion(bf16[512,4,16]{0,2,1:T(8,128)(2,1)S(1)} %bitcast.149, f32[4,512,1024]{2,1,0:T(8,128)} %fusion.155, f32[4,512,1024]{2,1,0:T(8,128)} %get-tuple-element.531, f32[4,512]{1,0:T(4,128)S(1)} %get-tuple-element.532), kind=kOutput, calls=%fused_computation.22.clone.1 | convolution fusion | flops 85986304 | bytes 17113088 | tf_op jit(solution)/shard_map/while/body/eval_jaxpr/while/body/eval_jaxpr/hqk,qhd->khd/dot_general | solution.py:129
  256.5 4.5 fusion.155
  261.0 4.7 fusion.156
  265.6 21.2 %fusion.157 = bf16[4,16,512]{2,1,0:T(8,128)(2,1)S(1)} fusion(bf16[1024,4,16]{0,2,1:T(8,128)(2,1)S(1)} %bitcast.144, f32[4,512,1024]{2,1,0:T(8,128)} %fusion.155, f32[4,512,1024]{2,1,0:T(8,128)} %get-tuple-element.531, f32[4,512]{1,0:T(4,128)S(1)} %get-tuple-element.532), kind=kOutput, calls=%fused_computation.23.clone.1 | convolution fusion | flops 85986304 | bytes 16982016 | tf_op jit(solution)/shard_map/while/body/eval_jaxpr/while/body/eval_jaxpr/hqk,khd->qhd/dot_general | solution.py:126
  291.1 18.5 %fusion.159 = f32[4,16,1024]{2,1,0:T(8,128)S(1)} fusion(bf16[512,4,16]{0,2,1:T(8,128)(2,1)S(1)} %bitcast.149, f32[4,512,1024]{2,1,0:T(8,128)} %fusion.155, f32[4,512,1024]{2,1,0:T(8,128)} %get-tuple-element.531, f32[4,512]{1,0:T(4,128)S(1)} %get-tuple-element.532), kind=kOutput, calls=%fused_computation.22.clone.1 | convolution fusion | flops 85986304 | bytes 17113088 | tf_op jit(solution)/shard_map/while/body/eval_jaxpr/while/body/eval_jaxpr/hqk,qhd->khd/dot_general | solution.py:129
  318.2 4.7 fusion.156
  322.9 21.2 %fusion.157 = bf16[4,16,512]{2,1,0:T(8,128)(2,1)S(1)} fusion(bf16[1024,4,16]{0,2,1:T(8,128)(2,1)S(1)} %bitcast.144, f32[4,512,1024]{2,1,0:T(8,128)} %fusion.155, f32[4,512,1024]{2,1,0:T(8,128)} %get-tuple-element.531, f32[4,512]{1,0:T(4,128)S(1)} %get-tuple-element.532), kind=kOutput, calls=%fused_computation.23.clone.1 | convolution fusion | flops 85986304 | bytes 16982016 | tf_op jit(solution)/shard_map/while/body/eval_jaxpr/while/body/eval_jaxpr/hqk,khd->qhd/dot_general | solution.py:126
  348.3 18.5 %fusion.159 = f32[4,16,1024]{2,1,0:T(8,128)S(1)} fusion(bf16[512,4,16]{0,2,1:T(8,128)(2,1)S(1)} %bitcast.149, f32[4,512,1024]{2,1,0:T(8,128)} %fusion.155, f32[4,512,1024]{2,1,0:T(8,128)} %get-tuple-element.531, f32[4,512]{1,0:T(4,128)S(1)} %get-tuple-element.532), kind=kOutput, calls=%fused_computation.22.clone.1 | convolution fusion | flops 85986304 | bytes 17113088 | tf_op jit(solution)/shard_map/while/body/eval_jaxpr/while/body/eval_jaxpr/hqk,qhd->khd/dot_general | solution.py:129
  377.1 228.9 %while.60 = (s32[]{:T(128)}, bf16[4,512,64]{1,2,0:T(8,128)(2,1)S(1)}, f32[4,1024,64]{1,2,0:T(8,128)}, f32[4,1024,64]{1,2,0:T(8,128)}, s32[4]{0:T(128)S(1)}, /*in...) while((s32[]{:T(128)}, ...), condition=%wide.region_13.13_spmd, body=%wide.region_10.12_spmd.sunk | while | flops 383782912 | bytes 61964504 | solution.py:202
  380.4 4.5 fusion.155
  384.9 4.7 fusion.156
  389.5 21.2 %fusion.157 = bf16[4,16,512]{2,1,0:T(8,128)(2,1)S(1)} fusion(bf16[1024,4,16]{0,2,1:T(8,128)(2,1)S(1)} %bitcast.144, f32[4,512,1024]{2,1,0:T(8,128)} %fusion.155, f32[4,512,1024]{2,1,0:T(8,128)} %get-tuple-element.531, f32[4,512]{1,0:T(4,128)S(1)} %get-tuple-element.532), kind=kOutput, calls=%fused_computation.23.clone.1 | convolution fusion | flops 85986304 | bytes 16982016 | tf_op jit(solution)/shard_map/while/body/eval_jaxpr/while/body/eval_jaxpr/hqk,khd->qhd/dot_general | solution.py:126
  415.0 18.5 %fusion.159 = f32[4,16,1024]{2,1,0:T(8,128)S(1)} fusion(bf16[512,4,16]{0,2,1:T(8,128)(2,1)S(1)} %bitcast.149, f32[4,512,1024]{2,1,0:T(8,128)} %fusion.155, f32[4,512,1024]{2,1,0:T(8,128)} %get-tuple-element.531, f32[4,512]{1,0:T(4,128)S(1)} %get-tuple-element.532), kind=kOutput, calls=%fused_computation.22.clone.1 | convolution fusion | flops 85986304 | bytes 17113088 | tf_op jit(solution)/shard_map/while/body/eval_jaxpr/while/body/eval_jaxpr/hqk,qhd->khd/dot_general | solution.py:129
  442.1 4.7 fusion.156
  446.8 21.2 %fusion.157 = bf16[4,16,512]{2,1,0:T(8,128)(2,1)S(1)} fusion(bf16[1024,4,16]{0,2,1:T(8,128)(2,1)S(1)} %bitcast.144, f32[4,512,1024]{2,1,0:T(8,128)} %fusion.155, f32[4,512,1024]{2,1,0:T(8,128)} %get-tuple-element.531, f32[4,512]{1,0:T(4,128)S(1)} %get-tuple-element.532), kind=kOutput, calls=%fused_computation.23.clone.1 | convolution fusion | flops 85986304 | bytes 16982016 | tf_op jit(solution)/shard_map/while/body/eval_jaxpr/while/body/eval_jaxpr/hqk,khd->qhd/dot_general | solution.py:126
  472.2 18.5 %fusion.159 = f32[4,16,1024]{2,1,0:T(8,128)S(1)} fusion(bf16[512,4,16]{0,2,1:T(8,128)(2,1)S(1)} %bitcast.149, f32[4,512,1024]{2,1,0:T(8,128)} %fusion.155, f32[4,512,1024]{2,1,0:T(8,128)} %get-tuple-element.531, f32[4,512]{1,0:T(4,128)S(1)} %get-tuple-element.532), kind=kOutput, calls=%fused_computation.22.clone.1 | convolution fusion | flops 85986304 | bytes 17113088 | tf_op jit(solution)/shard_map/while/body/eval_jaxpr/while/body/eval_jaxpr/hqk,qhd->khd/dot_general | solution.py:129
  494.8 4.5 fusion.155
  499.3 4.7 fusion.156
  504.0 21.2 %fusion.157 = bf16[4,16,512]{2,1,0:T(8,128)(2,1)S(1)} fusion(bf16[1024,4,16]{0,2,1:T(8,128)(2,1)S(1)} %bitcast.144, f32[4,512,1024]{2,1,0:T(8,128)} %fusion.155, f32[4,512,1024]{2,1,0:T(8,128)} %get-tuple-element.531, f32[4,512]{1,0:T(4,128)S(1)} %get-tuple-element.532), kind=kOutput, calls=%fused_computation.23.clone.1 | convolution fusion | flops 85986304 | bytes 16982016 | tf_op jit(solution)/shard_map/while/body/eval_jaxpr/while/body/eval_jaxpr/hqk,khd->qhd/dot_general | solution.py:126
  529.4 18.5 %fusion.159 = f32[4,16,1024]{2,1,0:T(8,128)S(1)} fusion(bf16[512,4,16]{0,2,1:T(8,128)(2,1)S(1)} %bitcast.149, f32[4,512,1024]{2,1,0:T(8,128)} %fusion.155, f32[4,512,1024]{2,1,0:T(8,128)} %get-tuple-element.531, f32[4,512]{1,0:T(4,128)S(1)} %get-tuple-element.532), kind=kOutput, calls=%fused_computation.22.clone.1 | convolution fusion | flops 85986304 | bytes 17113088 | tf_op jit(solution)/shard_map/while/body/eval_jaxpr/while/body/eval_jaxpr/hqk,qhd->khd/dot_general | solution.py:129
  556.5 4.7 fusion.156
  561.2 21.2 %fusion.157 = bf16[4,16,512]{2,1,0:T(8,128)(2,1)S(1)} fusion(bf16[1024,4,16]{0,2,1:T(8,128)(2,1)S(1)} %bitcast.144, f32[4,512,1024]{2,1,0:T(8,128)} %fusion.155, f32[4,512,1024]{2,1,0:T(8,128)} %get-tuple-element.531, f32[4,512]{1,0:T(4,128)S(1)} %get-tuple-element.532), kind=kOutput, calls=%fused_computation.23.clone.1 | convolution fusion | flops 85986304 | bytes 16982016 | tf_op jit(solution)/shard_map/while/body/eval_jaxpr/while/body/eval_jaxpr/hqk,khd->qhd/dot_general | solution.py:126
  586.6 18.5 %fusion.159 = f32[4,16,1024]{2,1,0:T(8,128)S(1)} fusion(bf16[512,4,16]{0,2,1:T(8,128)(2,1)S(1)} %bitcast.149, f32[4,512,1024]{2,1,0:T(8,128)} %fusion.155, f32[4,512,1024]{2,1,0:T(8,128)} %get-tuple-element.531, f32[4,512]{1,0:T(4,128)S(1)} %get-tuple-element.532), kind=kOutput, calls=%fused_computation.22.clone.1 | convolution fusion | flops 85986304 | bytes 17113088 | tf_op jit(solution)/shard_map/while/body/eval_jaxpr/while/body/eval_jaxpr/hqk,qhd->khd/dot_general | solution.py:129
  610.3 5.2 bitcast_reduce_fusion
  615.5 5.4 copy.55
  624.6 6.0 collective-permute-done.5
  630.5 5.5 collective-permute-done.4
  639.2 5.4 scatter_custom_fusion
  654.4 6.5 scatter_custom_fusion.1
  (245 shorter events, 147.9 us)
Async XLA Ops:
  0.6 110.4 %copy-start = (bf16[256,1024]{1,0:T(8,128)(2,1)S(1)}, bf16[256,1024]{1,0:T(8,128)(2,1)}, u32[]{:S(2)}) copy-start(bf16[256,1024]{1,0:T(8,128)(2,1)} %param.27) | copy-start | bytes 1572868
  0.6 19.8 %copy-start.5 = (bf16[1,1024,256]{2,1,0:T(8,128)(2,1)S(1)}, bf16[1,1024,256]{2,1,0:T(8,128)(2,1)}, u32[]{:S(2)}) copy-start(bf16[1,1024,256]{2,1,0:T(8,128)(2,1)} %param.20) | copy-start | bytes 1572868
  0.7 11.1 %copy-start.28 = (s32[1,1024]{1,0:T(1,128)S(1)}, s32[1,1024]{1,0:T(1,128)}, u32[]{:S(2)}) copy-start(s32[1,1024]{1,0:T(1,128)} %param.22) | copy-start | bytes 12292
  1.5 0.6 copy-start.26
  5.3 9.6 %collective-permute-start.1 = (bf16[384,256]{1,0:T(8,128)(2,1)S(1)}, bf16[384,256]{1,0:T(8,128)(2,1)S(1)}, u32[]{:S(2)}, u32[]{:S(2)}) collective-permute-start(bf16[384,256]{1,0:T(8,128)(2,1)S(1)} %get-tuple-element.352), channel_id=1, source_target_pairs={{1,0},{2,1},{3,2},{4,3},{5,4},{6,5},{7,6},{8,7},{9,8},{10,9},{11,1... | collective-permute-start | bytes 589832 | tf_op jit(solution)/shard_map/ppermute | solution.py:25
  11.7 8.7 %collective-permute-start = (bf16[384,256]{1,0:T(8,128)(2,1)S(1)}, bf16[384,256]{1,0:T(8,128)(2,1)S(1)}, u32[]{:S(2)}, u32[]{:S(2)}) collective-permute-start(bf16[384,256]{1,0:T(8,128)(2,1)S(1)} %get-tuple-element.351), channel_id=1, source_target_pairs={{0,1},{1,2},{2,3},{3,4},{4,5},{5,6},{6,7},{7,8},{8,9},{9,10},{10,1... | collective-permute-start | bytes 589832 | tf_op jit(solution)/shard_map/ppermute | solution.py:23
  11.7 3.2 copy-start.27
  11.8 13.8 %copy-start.30 = (bf16[256,768]{1,0:T(8,128)(2,1)S(1)}, bf16[256,768]{1,0:T(8,128)(2,1)}, u32[]{:S(2)}) copy-start(bf16[256,768]{1,0:T(8,128)(2,1)} %param.24) | copy-start | bytes 1179652
  11.8 13.8 %copy-start.33 = (f32[256]{0:T(256)S(1)}, f32[256]{0:T(256)}, u32[]{:S(2)}) copy-start(f32[256]{0:T(256)} %param.23) | copy-start | bytes 3076
  24.4 3.4 copy-start.16
  24.7 5.3 copy-start.6
  24.8 0.8 copy-start.18
  25.6 0.7 copy-start.22
  27.3 7.0 %collective-permute-start.3 = (bf16[512,512]{1,0:T(8,128)(2,1)}, bf16[512,512]{1,0:T(8,128)(2,1)}, u32[]{:S(2)}, u32[]{:S(2)}) collective-permute-start(bf16[512,512]{1,0:T(8,128)(2,1)} %get-tuple-element.348), channel_id=1, source_target_pairs={{1,0},{2,1},{3,2},{4,3},{5,4},{6,5},{7,6},{8,7},{9,8},{10,9},{11,1... | collective-permute-start | bytes 1572872 | tf_op jit(solution)/shard_map/ppermute | solution.py:25
  27.4 12.5 %collective-permute-start.2 = (bf16[512,512]{1,0:T(8,128)(2,1)}, bf16[512,512]{1,0:T(8,128)(2,1)}, u32[]{:S(2)}, u32[]{:S(2)}) collective-permute-start(bf16[512,512]{1,0:T(8,128)(2,1)} %get-tuple-element.347), channel_id=1, source_target_pairs={{0,1},{1,2},{2,3},{3,4},{4,5},{5,6},{6,7},{7,8},{8,9},{9,10},{10,1... | collective-permute-start | bytes 1572872 | tf_op jit(solution)/shard_map/ppermute | solution.py:23
  45.8 63.5 %copy-start.15 = (bf16[256,256]{1,0:T(8,128)(2,1)S(1)}, bf16[256,256]{1,0:T(8,128)(2,1)}, u32[]{:S(2)}) copy-start(bf16[256,256]{1,0:T(8,128)(2,1)} %param.25) | copy-start | bytes 393220
  45.8 65.2 %copy-start.32 = (f32[256]{0:T(256)S(1)}, f32[256]{0:T(256)}, u32[]{:S(2)}) copy-start(f32[256]{0:T(256)} %param.26) | copy-start | bytes 3076
  110.8 11.1 %copy-start.8 = (f32[1024,256]{0,1:T(8,128)}, f32[1024,256]{0,1:T(8,128)S(1)}, u32[]{:S(2)}) copy-start(f32[1024,256]{0,1:T(8,128)S(1)} %get-tuple-element.354) | copy-start | bytes 3145732
  121.9 10.2 %copy-start.12 = (bf16[1,1024,256]{1,2,0:T(8,128)(2,1)S(1)}, bf16[1,1024,256]{1,2,0:T(8,128)(2,1)}, u32[]{:S(2)}) copy-start(bf16[1,1024,256]{1,2,0:T(8,128)(2,1)} %copy.50) | copy-start | bytes 1572868
  131.2 1.0 copy-start.10
  131.2 2.2 copy-start.24
  133.4 4.3 copy-start.35
  133.4 5.4 copy-start.2
  367.7 4.0 copy-start.3
  367.7 4.0 copy-start.36
  371.7 4.3 copy-start.35
  371.7 5.4 copy-start.2
  606.0 4.0 copy-start.3
  606.0 4.0 copy-start.36
  620.9 3.4 copy-start.4
  623.6 6.9 %collective-permute-start.5 = (bf16[512,512]{1,0:T(8,128)(2,1)S(1)}, bf16[512,512]{1,0:T(8,128)(2,1)S(1)}, u32[]{:S(2)}, u32[]{:S(2)}) collective-permute-start(bf16[512,512]{1,0:T(8,128)(2,1)S(1)} %get-tuple-element.346), channel_id=1, source_target_pairs={{1,0},{2,1},{3,2},{4,3},{5,4},{6,5},{7,6},{8,7},{9,8},{10,9},{11,1... | collective-permute-start | bytes 1572872 | tf_op jit(solution)/shard_map/ppermute | solution.py:25
  623.8 12.2 %collective-permute-start.4 = (bf16[512,512]{1,0:T(8,128)(2,1)S(1)}, bf16[512,512]{1,0:T(8,128)(2,1)S(1)}, u32[]{:S(2)}, u32[]{:S(2)}) collective-permute-start(bf16[512,512]{1,0:T(8,128)(2,1)S(1)} %get-tuple-element.345), channel_id=1, source_target_pairs={{0,1},{1,2},{2,3},{3,4},{4,5},{5,6},{6,7},{7,8},{8,9},{9,10},{10,1... | collective-permute-start | bytes 1572872 | tf_op jit(solution)/shard_map/ppermute | solution.py:23
  636.2 1.0 copy-start.7
  636.2 1.0 copy-start.19
  636.2 1.2 copy-start.29
  636.2 1.3 copy-start.31
  636.2 1.3 copy-start.34
  636.5 1.7 copy-start.21
  636.5 1.7 copy-start.23
  636.7 1.8 copy-start.11
  636.7 1.8 copy-start.13
  636.7 1.8 copy-start.25
  638.1 7.7 %copy-start.9 = (f32[1024,256]{0,1:T(8,128)S(1)}, f32[1024,256]{0,1:T(8,128)}, u32[]{:S(2)}) copy-start(f32[1024,256]{0,1:T(8,128)} %copy-done.8) | copy-start | bytes 3145732
  638.2 7.7 %copy-start.14 = (bf16[1024,256]{1,0:T(8,128)(2,1)S(1)}, bf16[1024,256]{1,0:T(8,128)(2,1)}, u32[]{:S(2)}) copy-start(bf16[1024,256]{1,0:T(8,128)(2,1)} %param.28) | copy-start | bytes 1572868
  645.3 5.8 collective-permute-start.7
  645.4 16.3 %copy-start.1 = (bf16[256,1024]{1,0:T(8,128)(2,1)S(1)}, bf16[256,1024]{1,0:T(8,128)(2,1)}, u32[]{:S(2)}) copy-start(bf16[256,1024]{1,0:T(8,128)(2,1)} %param.27) | copy-start | bytes 1572868
  645.4 9.0 %collective-permute-start.6 = (bf16[384,256]{1,0:T(8,128)(2,1)}, bf16[384,256]{1,0:T(8,128)(2,1)}, u32[]{:S(2)}, u32[]{:S(2)}) collective-permute-start(bf16[384,256]{1,0:T(8,128)(2,1)} %get-tuple-element.349), channel_id=1, source_target_pairs={{0,1},{1,2},{2,3},{3,4},{4,5},{5,6},{6,7},{7,8},{8,9},{9,10},{10,1... | collective-permute-start | bytes 589832 | tf_op jit(solution)/shard_map/ppermute | solution.py:23
  660.9 0.8 copy-start.17
  (1 other events, 0.6 us)
where the time goes:
time: 663 us; the launch traced here: 662 us
  matrix products  506 us (76%)
  local copies, waits for them, and re-layouts  75.1 us (11%)
  waiting for transfers between devices  32.3 us (5%)
  other arithmetic  28 us (4%)
  loops' own time  11.4 us (2%)
  starting transfers between devices  8.01 us (1%)
    dot_general x8, matrix products, attend_backward(): jnp.einsum('hqk,khd->qhd', grad_scores, key_heads, preferred_element_type...  169 us
    dot_general x8, matrix products, attend_backward(): jnp.einsum('hqk,qhd->khd', grad_scores, query_heads, preferred_element_ty...  148 us
    dot_general x8, matrix products, attend_backward(): jnp.einsum('qhd,khd->hqk', query_heads, key_heads, preferred_element_type...  37.2 us
    dot_general x8, matrix products, attend_backward(): jnp.einsum('qhd,khd->hqk', grad_heads, value_heads, preferred_element_typ...  36 us
    dot_general x8, matrix products, attend_backward(): jnp.einsum('hqk,qhd->khd', probs_b, grad_heads, preferred_element_type=jn...  34 us
    dot_general x2, matrix products, attend(): jnp.einsum('qhd,khd->hqk', query_heads, key_heads, preferred_element_type...  27.2 us
    dot_general x2, matrix products, attend(): jnp.einsum('hqk,khd->qhd', probs_b, value_heads, preferred_element_type=j...  26.8 us
    ppermute x4, waiting for transfers between devices, with_halo(): lax.ppermute(tail, axis, [(i, (i + 1) % count) for i in range(count)])  19.8 us
  transfers between devices with their start and end apart: 8, of which 7 were waited for; matrix products, arithmetic and copies ran while one was open for 1% of the time, Pallas kernels for 0%

commit v1 on v0

v1 whole, which is shorter than its diff:
```python
import functools
import math

import jax
import jax.numpy as jnp
from jax import lax
from jax.experimental import pallas as pl
from jax.experimental.pallas import tpu as pltpu
from jax.sharding import PartitionSpec as P

H = 16
SHIFT = 512
CHUNK = 256
EPS = 1e-05
AXES = ("gx", "gy")
F32 = jnp.float32
BF16 = jnp.bfloat16
VMEM = pl.BlockSpec(memory_space=pltpu.VMEM)


def mm(a, b):
    return lax.dot_general(a, b, (((1,), (0,)), ((), ())), preferred_element_type=F32)


def mm_t(a, b):
    return lax.dot_general(a, b, (((1,), (1,)), ((), ())), preferred_element_type=F32)


def normalize(rows):
    centered = rows - jnp.mean(rows, axis=-1, keepdims=True)
    inv = lax.rsqrt(jnp.mean(centered * centered, axis=-1, keepdims=True) + EPS)
    return centered * inv, inv


def normalize_back(unit, inv, grad):
    inner = jnp.mean(grad * unit, axis=-1, keepdims=True)
    return inv * (grad - jnp.mean(grad, axis=-1, keepdims=True) - unit * inner)


def as_column(row):
    wide = jnp.broadcast_to(row.astype(F32), (8, row.shape[1]))
    return wide.T[:, :1].astype(jnp.int32)


def pick(column, first, count):
    ids = lax.broadcasted_iota(jnp.int32, (column.shape[0], count), 1) + first
    return (column == ids).astype(F32).astype(BF16)


def place(row, first, count):
    ids = lax.broadcasted_iota(jnp.int32, (count, row.shape[1]), 0) + first
    return (row == ids).astype(F32).astype(BF16)


def outgoing_kernel(points_ref, send_ref, out_ref):
    out_ref[...] = mm(pick(as_column(send_ref[...]), 0, points_ref.shape[0]), points_ref[...]).astype(BF16)


def order_kernel(points_ref, prev_ref, next_ref, slot_ref, out_ref):
    rows, cap = points_ref.shape[0], prev_ref.shape[0]
    column = as_column(slot_ref[...])
    for start in range(0, rows, CHUNK):
        part = column[start : start + CHUNK]
        total = mm(pick(part, 0, rows), points_ref[...])
        total += mm(pick(part, rows, cap), prev_ref[...])
        total += mm(pick(part, rows + cap, cap), next_ref[...])
        out_ref[start : start + CHUNK, :] = total.astype(BF16)


def back_kernel(grad_ref, slot_ref, out_ref):
    out_ref[...] = mm(place(slot_ref[...], grad_ref.shape[0], out_ref.shape[0]), grad_ref[...]).astype(BF16)


def final_kernel(grad_ref, slot_ref, send_ref, prev_ref, next_ref, out_ref):
    rows, cap = grad_ref.shape[0], prev_ref.shape[0]
    for start in range(0, rows, CHUNK):
        total = mm(place(slot_ref[...], start, CHUNK), grad_ref[...])
        total += mm(place(send_ref[:, :cap], start, CHUNK), prev_ref[...])
        total += mm(place(send_ref[:, cap:], start, CHUNK), next_ref[...])
        out_ref[start : start + CHUNK, :] = total.astype(BF16)


def block_kernel(
    x_ref, cot_ref, gain1_ref, wqkv_ref, proj_ref, gain2_ref, fc1_ref, fc2_ref,
    out_ref, grad_ref,
    exps, q3, k3, v3, attn, recip, gext, gmixed, dqkv,
):
    rows, width = x_ref.shape
    hd = proj_ref.shape[0]
    head = hd // H
    scale = 1.0 / math.sqrt(head)
    starts = range(0, rows, CHUNK)
    wqkv_t = wqkv_ref[...].T
    tail = lax.broadcasted_iota(jnp.int32, (H, head, rows), 1)
    v3[:, head:, :] = jnp.where(tail < 2, 1.0, 0.0).astype(BF16)

    for start in starts:
        part = slice(start, start + CHUNK)
        unit, inv = normalize(x_ref[part, :].astype(F32))
        qkv = mm_t(wqkv_t, (unit * gain1_ref[...]).astype(BF16)).astype(BF16)
        q3[:, :, part] = (qkv[:hd].astype(F32) * scale).astype(BF16).reshape(H, head, CHUNK)
        k3[:, :, part] = qkv[hd : 2 * hd].reshape(H, head, CHUNK)
        v3[:, :head, part] = qkv[2 * hd :].reshape(H, head, CHUNK)

    def forward_head(h, carry):
        q_rows = q3[h].T
        v_rows = v3[h].T
        keys = k3[h]
        for start in starts:
            part = slice(start, start + CHUNK)
            weights = jnp.exp(mm(q_rows[part], keys)).astype(BF16)
            exps[h, part, :] = weights
            summed = mm(weights, v_rows).T
            inverse = 1.0 / summed[head : head + 1]
            attn[h, :, part] = summed[:head] * inverse
            recip[h, :, part] = inverse
        return carry

    lax.fori_loop(0, H, forward_head, 0)

    for start in starts:
        part = slice(start, start + CHUNK)
        attn_t = attn[:, :, part].reshape(hd, CHUNK)
        mixed = x_ref[part, :].astype(F32) + mm(attn_t.T.astype(BF16), proj_ref[...])
        unit, inv = normalize(mixed)
        pre = mm((unit * gain2_ref[...]).astype(BF16), fc1_ref[...])
        half = 0.5 + 0.5 * lax.erf(pre * math.sqrt(0.5))
        out_ref[part, :] = (mixed + mm((pre * half).astype(BF16), fc2_ref[...])).astype(BF16)
        slope = half + pre * (math.sqrt(0.5 / math.pi) * jnp.exp(-0.5 * pre * pre))
        cot = cot_ref[part, :]
        grad_pre = (mm_t(cot, fc2_ref[...]) * slope).astype(BF16)
        grad_normed = mm_t(grad_pre, fc1_ref[...]) * gain2_ref[...]
        grad_mixed = cot.astype(F32) + normalize_back(unit, inv, grad_normed)
        gmixed[part, :] = grad_mixed
        grad_attn = mm_t(proj_ref[...], grad_mixed.astype(BF16)).astype(BF16).astype(F32)
        inverse = recip[:, :, part]
        inner = jnp.sum((grad_attn * attn_t).reshape(H, head, CHUNK), axis=1, keepdims=True) * inverse
        inner_hi = inner.astype(BF16).astype(F32)
        gext[:, :head, part] = (grad_attn.reshape(H, head, CHUNK) * inverse).astype(BF16)
        which = lax.broadcasted_iota(jnp.int32, (H, head, CHUNK), 1)
        rest = jnp.where(which == 0, -inner_hi, jnp.where(which == 1, inner_hi - inner, 0.0))
        gext[:, head:, part] = rest.astype(BF16)

    def backward_head(h, carry):
        g_rows = gext[h].T
        k_rows = k3[h].T
        values = v3[h]
        grad_k = jnp.zeros((head, rows), F32)
        grad_v = jnp.zeros((head, rows), F32)
        for start in starts:
            part = slice(start, start + CHUNK)
            weights = exps[h, part, :]
            scores = (weights.astype(F32) * mm(g_rows[part], values)).astype(BF16)
            grad_v += mm(gext[h, :head, part], weights)
            grad_k += mm(q3[h, :, part], scores)
            dqkv[h, :, part] = (mm(scores, k_rows).T * scale).astype(BF16)
        dqkv[H + h] = grad_k.astype(BF16)
        dqkv[2 * H + h] = grad_v.astype(BF16)
        return carry

    lax.fori_loop(0, H, backward_head, 0)

    for start in starts:
        part = slice(start, start + CHUNK)
        grad_qkv = dqkv[:, :, part].reshape(3 * hd, CHUNK).astype(F32).T.astype(BF16)
        grad_normed = mm_t(grad_qkv, wqkv_ref[...]) * gain1_ref[...]
        unit, inv = normalize(x_ref[part, :].astype(F32))
        grad_ref[part, :] = (gmixed[part, :] + normalize_back(unit, inv, grad_normed)).astype(BF16)


def call(kernel, outs, args, scratch=(), vmem=32):
    return pl.pallas_call(
        kernel,
        out_shape=outs,
        in_specs=[VMEM] * len(args),
        out_specs=jax.tree.map(lambda leaf: VMEM, outs),
        scratch_shapes=list(scratch),
        compiler_params=pltpu.CompilerParams(vmem_limit_bytes=vmem * 2**20),
    )(*args)


def shards(points, send_rows, recv_slot, gain1, wqkv, proj, gain2, fc1, fc2, cotangent):
    rows, width = points.shape[1:]
    cap = send_rows.shape[2] // 2
    hd = proj.shape[0]
    head = hd // H
    count = lax.axis_size(AXES)
    up = [(i, (i + 1) % count) for i in range(count)]
    down = [((i + 1) % count, i) for i in range(count)]
    local, send, slot, cot = points[0], send_rows[0], recv_slot, cotangent[0]

    def like(*shape):
        return jax.ShapeDtypeStruct(shape, BF16)

    cot_half = lax.ppermute(cot[SHIFT:], AXES, up)
    outgoing = call(outgoing_kernel, like(2 * cap, width), (local, send))
    from_prev = lax.ppermute(outgoing[cap:], AXES, up)
    from_next = lax.ppermute(outgoing[:cap], AXES, down)
    ordered = call(order_kernel, like(rows, width), (local, from_prev, from_next, slot))
    half = lax.ppermute(ordered[SHIFT:], AXES, up)
    patch = jnp.concatenate([half, ordered[:SHIFT]], axis=0)
    patch_cot = jnp.concatenate([cot_half, cot[:SHIFT]], axis=0)
    patch_out, patch_grad = call(
        block_kernel,
        (like(rows, width), like(rows, width)),
        (patch, patch_cot, gain1[None], wqkv, proj, gain2[None], fc1, fc2),
        (
            pltpu.VMEM((H, rows, rows), BF16),
            pltpu.VMEM((H, head, rows), BF16),
            pltpu.VMEM((H, head, rows), BF16),
            pltpu.VMEM((H, 2 * head, rows), BF16),
            pltpu.VMEM((H, head, rows), F32),
            pltpu.VMEM((H, 1, rows), F32),
            pltpu.VMEM((H, 2 * head, rows), BF16),
            pltpu.VMEM((rows, width), F32),
            pltpu.VMEM((3 * H, head, rows), BF16),
        ),
        vmem=60,
    )
    block_out = jnp.concatenate([patch_out[SHIFT:], lax.ppermute(patch_out[:SHIFT], AXES, down)], axis=0)
    grad = jnp.concatenate([patch_grad[SHIFT:], lax.ppermute(patch_grad[:SHIFT], AXES, down)], axis=0)
    back = call(back_kernel, like(2 * cap, width), (grad, slot))
    back_prev = lax.ppermute(back[cap:], AXES, up)
    back_next = lax.ppermute(back[:cap], AXES, down)
    grad_points = call(final_kernel, like(rows, width), (grad, slot, send, back_prev, back_next))
    return block_out[None], grad_points[None]


def solution(mesh):
    split = P(None, AXES, None)
    in_specs = (split, split, P(None, AXES), P(), P(), P(), P(), P(), P(), split)
    return jax.shard_map(shards, mesh=mesh, in_specs=in_specs, out_specs=(split, split), check_vma=False)
```

time: 663 us -> 119 us (0.18)
  matrix products: 506 us -> 0 us
  local copies, waits for them, and re-layouts: 75.1 us -> 3.02 us
  Pallas kernels: 0 us -> 71.1 us
  other arithmetic: 28 us -> 2.52 us
  loops' own time: 11.4 us -> 0 us
    dot_general x51 -> x0, matrix products: 506 us -> none  [the longest x8 169 us: attend_backward(): jnp.einsum('hqk,khd->qhd', grad_scores, key_heads, preferred_element_type...]
    pallas_call x0 -> x5, Pallas kernels: none -> 71.1 us  [call(): pl.pallas_call(kernel, out_shape=outs, in_specs=[VMEM] * len(args), out_s...]
    dynamic_slice x52 -> x0, local copies, waits for them, and re-layouts: 29.1 us -> none  [the longest x32 14.9 us: columns(): return lax.dynamic_slice_in_dim(matrix, start, group_width, 1)]
    another operation x4 -> x0, loops' own time: 11.4 us -> none  [the longest x2 5.82 us: backward_block(): lax.map(one_group, jnp.arange(group_count, dtype=jnp.int32))]
    dynamic_update_slice x24 -> x0, local copies, waits for them, and re-layouts: 10.4 us -> none  [the longest x16 6.93 us: backward_block(): lax.map(one_group, jnp.arange(group_count, dtype=jnp.int32))]
    reduce_sum x6 -> x0, other arithmetic: 7.67 us -> none  [the longest x1 5.22 us: shards(): paired.reshape(block_count // 2 + 1, 2, K, 2 * head_width).sum(axis=1)]
    gather x3 -> x0, local copies, waits for them, and re-layouts: 7.35 us -> none  [the longest x2 4.15 us: shards(): ordered = pool[slot_index]]
    scatter-add x3 -> x0, other arithmetic: 6.92 us -> none  [the longest x1 6.48 us: shards(): grad_event = back_pool[:row_count].at[sender].add(returned_rows)]
  transfers between devices with their start and end apart: 8 -> 8, of which waited for: 7 -> 7; matrix products, arithmetic and copies ran while one was open for 1% -> 2% of each run, Pallas kernels for 0% -> 2%
where the time goes in v1:
time: 119 us
  Pallas kernels  71.1 us (60%)
  waiting for transfers between devices  28.7 us (24%)
  starting transfers between devices  12.5 us (11%)
  local copies, waits for them, and re-layouts  3.02 us (3%)
  other arithmetic  2.52 us (2%)
    pallas_call x5, Pallas kernels, call(): pl.pallas_call(kernel, out_shape=outs, in_specs=[VMEM] * len(args), out_s...  71.1 us
    ppermute x1, waiting for transfers between devices, shards(): half = lax.ppermute(ordered[SHIFT:], AXES, up)  7.51 us
    ppermute x1, starting transfers between devices, shards(): from_next = lax.ppermute(outgoing[:cap], AXES, down)  6.42 us
    ppermute x1, starting transfers between devices, shards(): back_next = lax.ppermute(back[:cap], AXES, down)  5.65 us
    ppermute x1, waiting for transfers between devices, shards(): from_prev = lax.ppermute(outgoing[cap:], AXES, up)  5.5 us
    ppermute x1, waiting for transfers between devices, shards(): back_prev = lax.ppermute(back[cap:], AXES, up)  5.5 us
    ppermute x1, waiting for transfers between devices, shards(): lax.ppermute(patch_grad[:SHIFT], AXES, down)  3.76 us
    ppermute x1, waiting for transfers between devices, shards(): from_next = lax.ppermute(outgoing[:cap], AXES, down)  3.08 us
  transfers between devices with their start and end apart: 8, of which 7 were waited for; matrix products, arithmetic and copies ran while one was open for 2% of the time, Pallas kernels for 2%

profile of v1, /device:TPU:0, one launch (start us, length us, event | category | flops | bytes accessed | tf_op | source)
XLA Modules:
  0.0 118.7 jit_solution(15195034218305906616)
XLA Ops:
  0.6 0.0 copy-start.2
  0.6 0.7 copy-done.2
  1.3 0.0 copy-start
  1.3 1.0 copy-done
  2.4 0.9 shard_map.113
  3.2 0.0 copy-start.3
  3.3 6.4 %collective-permute-start.1 = (bf16[384,256]{1,0:T(8,128)(2,1)S(1)}, bf16[384,256]{1,0:T(8,128)(2,1)S(1)}, u32[]{:S(2)}, u32[]{:S(2)}) collective-permute-start(bf16[384,256]{1,0:T(8,128)(2,1)S(1)} %get-tuple-element.16), channel_id=1, source_target_pairs={{1,0},{2,1},{3,2},{4,3},{5,4},{6,5},{7,6},{8,7},{9,8},{10,9},{11,1... | collective-permute-start | bytes 589832 | tf_op jit(solution)/shard_map/ppermute | solution.py:198
  9.7 0.0 collective-permute-start
  9.7 0.0 copy-done.3
  9.7 0.0 copy-start.1
  9.7 0.1 collective-permute-start.3
  9.8 3.1 %collective-permute-done.1.next_ref = bf16[384,256]{1,0:T(8,128)(2,1)S(1)} collective-permute-done((bf16[384,256]{1,0:T(8,128)(2,1)S(1)}, bf16[384,256]{1,0:T(8,128)(2,1)S(1)}, u32[]{:S(2)}, u32[]{:S(2)}) %collective-permute-start.1) | collective-permute-done | bytes 196640 | tf_op jit(solution)/shard_map/ppermute | solution.py:198
  12.9 5.5 %collective-permute-done.prev_ref = bf16[384,256]{1,0:T(8,128)(2,1)S(1)} collective-permute-done((bf16[384,256]{1,0:T(8,128)(2,1)S(1)}, bf16[384,256]{1,0:T(8,128)(2,1)S(1)}, u32[]{:S(2)}, u32[]{:S(2)}) %collective-permute-start) | collective-permute-done | bytes 196640 | tf_op jit(solution)/shard_map/ppermute | solution.py:197
  18.4 0.0 copy-done.1
  18.4 1.5 %shard_map.114 = bf16[1024,256]{1,0:T(8,128)(2,1)S(1)} custom-call(bf16[1024,256]{1,0:T(8,128)(2,1)S(1)} %bitcast.12, bf16[384,256]{1,0:T(8,128)(2,1)S(1)} %collective-permute-done.prev_ref, bf16[384,256]{1,0:T(8,128)(2,1)S(1)} %collective-permute-done.1.next_ref, s32[1,1024]{1,0:T(1,128)S(1)} %copy-done.1), custom_call_target="tpu_custom_call" | custom-call | tf_op jit(solution)/shard_map/pallas_call | solution.py:172
  19.9 0.2 collective-permute-start.2
  20.1 1.0 collective-permute-done.3
  21.2 0.8 pad_maximum_fusion.1.cot_ref
  22.0 7.5 %collective-permute-done.2 = bf16[512,256]{1,0:T(8,128)(2,1)S(1)} collective-permute-done((bf16[512,256]{1,0:T(8,128)(2,1)S(1)}, bf16[512,256]{1,0:T(8,128)(2,1)S(1)}, u32[]{:S(2)}, u32[]{:S(2)}) %collective-permute-start.2) | collective-permute-done | bytes 262176 | tf_op jit(solution)/shard_map/ppermute | solution.py:200
  29.5 0.8 pad_maximum_fusion.x_ref
  30.4 66.2 %shard_map.115 = (bf16[1024,256]{1,0:T(8,128)(2,1)}, bf16[1024,256]{1,0:T(8,128)(2,1)}) custom-call(bf16[1024,256]{1,0:T(8,128)(2,1)} %pad_maximum_fusion.x_ref, bf16[1024,256]{1,0:T(8,128)(2,1)} %pad_maximum_fusion.1.cot_ref, f32[1,256]{1,0:T(1,128)} %bitcast.16, bf16[256,768]{1,0:T(8,128)(2,1)} %wqkv_ref.1, bf16[256,256]{1,0:T(8,128)(2,1)} %proj_ref.1, ...), custom_call_target="tpu_custom_call" | custom-call | tf_op jit(solution)/shard_map/pallas_call | solution.py:172
  96.6 0.0 copy-start.4
  96.6 1.1 fusion
  97.7 0.1 collective-permute-start.5
  97.8 0.0 copy-done.4
  97.8 0.1 collective-permute-start.4
  97.9 3.8 %collective-permute-done.5 = bf16[512,256]{1,0:T(8,128)(2,1)S(1)} collective-permute-done((bf16[512,256]{1,0:T(8,128)(2,1)S(1)}, bf16[512,256]{1,0:T(8,128)(2,1)S(1)}, u32[]{:S(2)}, u32[]{:S(2)}) %collective-permute-start.5) | collective-permute-done | bytes 262176 | tf_op jit(solution)/shard_map/ppermute | solution.py:221
  101.7 0.6 shard_map.116
  102.3 5.7 %collective-permute-start.7 = (bf16[384,256]{1,0:T(8,128)(2,1)S(1)}, bf16[384,256]{1,0:T(8,128)(2,1)S(1)}, u32[]{:S(2)}, u32[]{:S(2)}) collective-permute-start(bf16[384,256]{1,0:T(8,128)(2,1)S(1)} %get-tuple-element.14), channel_id=1, source_target_pairs={{1,0},{2,1},{3,2},{4,3},{5,4},{6,5},{7,6},{8,7},{9,8},{10,9},{11,1... | collective-permute-start | bytes 589832 | tf_op jit(solution)/shard_map/ppermute | solution.py:224
  107.9 0.0 collective-permute-start.6
  108.0 0.0 collective-permute-done.4
  108.0 0.8 maximum_bitcast_fusion
  108.8 2.4 %collective-permute-done.7.next_ref = bf16[384,256]{1,0:T(8,128)(2,1)S(1)} collective-permute-done((bf16[384,256]{1,0:T(8,128)(2,1)S(1)}, bf16[384,256]{1,0:T(8,128)(2,1)S(1)}, u32[]{:S(2)}, u32[]{:S(2)}) %collective-permute-start.7) | collective-permute-done | bytes 196640 | tf_op jit(solution)/shard_map/ppermute | solution.py:224
  111.1 5.5 %collective-permute-done.6.prev_ref = bf16[384,256]{1,0:T(8,128)(2,1)S(1)} collective-permute-done((bf16[384,256]{1,0:T(8,128)(2,1)S(1)}, bf16[384,256]{1,0:T(8,128)(2,1)S(1)}, u32[]{:S(2)}, u32[]{:S(2)}) %collective-permute-start.6) | collective-permute-done | bytes 196640 | tf_op jit(solution)/shard_map/ppermute | solution.py:223
  116.6 2.0 %shard_map.117 = bf16[1024,256]{1,0:T(8,128)(2,1)} custom-call(bf16[1024,256]{1,0:T(8,128)(2,1)S(1)} %pad_maximum_fusion.2.grad_ref, s32[1,1024]{1,0:T(1,128)S(1)} %copy-done.1, s32[1,768]{1,0:T(1,128)S(1)} %bitcast.14, bf16[384,256]{1,0:T(8,128)(2,1)S(1)} %collective-permute-done.6.prev_ref, bf16[384,256]{1,0:T(8,128)(2,1)S(1)} %collective-permute-done.7.next_ref), custom_call_target="tpu_custom_call" | custom-call | tf_op jit(solution)/shard_map/pallas_call | solution.py:172
  (6 shorter events, 0.2 us)
Async XLA Ops:
  0.6 0.7 copy-start.2
  1.3 1.0 copy-start
  3.2 6.5 %copy-start.3 = (bf16[1,1024,256]{2,1,0:T(8,128)(2,1)S(1)}, bf16[1,1024,256]{2,1,0:T(8,128)(2,1)}, u32[]{:S(2)}) copy-start(bf16[1,1024,256]{2,1,0:T(8,128)(2,1)} %param.19) | copy-start | bytes 1572868
  3.3 9.6 %collective-permute-start.1 = (bf16[384,256]{1,0:T(8,128)(2,1)S(1)}, bf16[384,256]{1,0:T(8,128)(2,1)S(1)}, u32[]{:S(2)}, u32[]{:S(2)}) collective-permute-start(bf16[384,256]{1,0:T(8,128)(2,1)S(1)} %get-tuple-element.16), channel_id=1, source_target_pairs={{1,0},{2,1},{3,2},{4,3},{5,4},{6,5},{7,6},{8,7},{9,8},{10,9},{11,1... | collective-permute-start | bytes 589832 | tf_op jit(solution)/shard_map/ppermute | solution.py:198
  9.7 8.7 %collective-permute-start = (bf16[384,256]{1,0:T(8,128)(2,1)S(1)}, bf16[384,256]{1,0:T(8,128)(2,1)S(1)}, u32[]{:S(2)}, u32[]{:S(2)}) collective-permute-start(bf16[384,256]{1,0:T(8,128)(2,1)S(1)} %get-tuple-element.17), channel_id=1, source_target_pairs={{0,1},{1,2},{2,3},{3,4},{4,5},{5,6},{6,7},{7,8},{8,9},{9,10},{10,1... | collective-permute-start | bytes 589832 | tf_op jit(solution)/shard_map/ppermute | solution.py:197
  9.7 8.7 %copy-start.1 = (s32[1,1024]{1,0:T(1,128)S(1)}, s32[1,1024]{1,0:T(1,128)}, u32[]{:S(2)}) copy-start(s32[1,1024]{1,0:T(1,128)} %slot_ref.5) | copy-start | bytes 12292
  9.7 11.5 %collective-permute-start.3 = (bf16[512,256]{1,0:T(8,128)(2,1)S(1)}, bf16[512,256]{1,0:T(8,128)(2,1)S(1)}, u32[]{:S(2)}, u32[]{:S(2)}) collective-permute-start(bf16[512,256]{1,0:T(8,128)(2,1)S(1)} %get-tuple-element.10), channel_id=1, source_target_pairs={{0,1},{1,2},{2,3},{3,4},{4,5},{5,6},{6,7},{7,8},{8,9},{9,10},{10,1... | collective-permute-start | bytes 786440 | tf_op jit(solution)/shard_map/ppermute | solution.py:195
  19.9 9.6 %collective-permute-start.2 = (bf16[512,256]{1,0:T(8,128)(2,1)S(1)}, bf16[512,256]{1,0:T(8,128)(2,1)S(1)}, u32[]{:S(2)}, u32[]{:S(2)}) collective-permute-start(bf16[512,256]{1,0:T(8,128)(2,1)S(1)} %get-tuple-element.12), channel_id=1, source_target_pairs={{0,1},{1,2},{2,3},{3,4},{4,5},{5,6},{6,7},{7,8},{8,9},{9,10},{10,1... | collective-permute-start | bytes 786440 | tf_op jit(solution)/shard_map/ppermute | solution.py:200
  96.6 1.2 %copy-start.4 = (bf16[1024,256]{1,0:T(8,128)(2,1)S(1)}, bf16[1024,256]{1,0:T(8,128)(2,1)}, u32[]{:S(2)}) copy-start(bf16[1024,256]{1,0:T(8,128)(2,1)} %get-tuple-element.4) | copy-start | bytes 1572868
  97.7 3.9 %collective-permute-start.5 = (bf16[512,256]{1,0:T(8,128)(2,1)S(1)}, bf16[512,256]{1,0:T(8,128)(2,1)S(1)}, u32[]{:S(2)}, u32[]{:S(2)}) collective-permute-start(bf16[512,256]{1,0:T(8,128)(2,1)S(1)} %get-tuple-element.7), channel_id=1, source_target_pairs={{1,0},{2,1},{3,2},{4,3},{5,4},{6,5},{7,6},{8,7},{9,8},{10,9},{11,1... | collective-permute-start | bytes 786440 | tf_op jit(solution)/shard_map/ppermute | solution.py:221
  97.8 10.1 %collective-permute-start.4 = (bf16[512,256]{1,0:T(8,128)(2,1)S(1)}, bf16[512,256]{1,0:T(8,128)(2,1)S(1)}, u32[]{:S(2)}, u32[]{:S(2)}) collective-permute-start(bf16[512,256]{1,0:T(8,128)(2,1)S(1)} %get-tuple-element.9), channel_id=1, source_target_pairs={{1,0},{2,1},{3,2},{4,3},{5,4},{6,5},{7,6},{8,7},{9,8},{10,9},{11,1... | collective-permute-start | bytes 786440 | tf_op jit(solution)/shard_map/ppermute | solution.py:220
  102.3 8.8 %collective-permute-start.7 = (bf16[384,256]{1,0:T(8,128)(2,1)S(1)}, bf16[384,256]{1,0:T(8,128)(2,1)S(1)}, u32[]{:S(2)}, u32[]{:S(2)}) collective-permute-start(bf16[384,256]{1,0:T(8,128)(2,1)S(1)} %get-tuple-element.14), channel_id=1, source_target_pairs={{1,0},{2,1},{3,2},{4,3},{5,4},{6,5},{7,6},{8,7},{9,8},{10,9},{11,1... | collective-permute-start | bytes 589832 | tf_op jit(solution)/shard_map/ppermute | solution.py:224
  107.9 8.7 %collective-permute-start.6 = (bf16[384,256]{1,0:T(8,128)(2,1)S(1)}, bf16[384,256]{1,0:T(8,128)(2,1)S(1)}, u32[]{:S(2)}, u32[]{:S(2)}) collective-permute-start(bf16[384,256]{1,0:T(8,128)(2,1)S(1)} %get-tuple-element.15), channel_id=1, source_target_pairs={{0,1},{1,2},{2,3},{3,4},{4,5},{5,6},{6,7},{7,8},{8,9},{9,10},{10,1... | collective-permute-start | bytes 589832 | tf_op jit(solution)/shard_map/ppermute | solution.py:223

commit v2 on v1

--- a/solution.py
+++ b/solution.py
@@ -16,6 +16,7 @@
 F32 = jnp.float32
 BF16 = jnp.bfloat16
 VMEM = pl.BlockSpec(memory_space=pltpu.VMEM)
+MESH = pl.DeviceIdType.MESH
 
 
 def mm(a, b):
@@ -52,32 +53,105 @@
     return (row == ids).astype(F32).astype(BF16)
 
 
-def outgoing_kernel(points_ref, send_ref, out_ref):
-    out_ref[...] = mm(pick(as_column(send_ref[...]), 0, points_ref.shape[0]), points_ref[...]).astype(BF16)
-
-
-def order_kernel(points_ref, prev_ref, next_ref, slot_ref, out_ref):
-    rows, cap = points_ref.shape[0], prev_ref.shape[0]
+def ring(sizes):
+    major, minor = sizes
+    count = major * minor
+    me = lax.axis_index("gx") * minor + lax.axis_index("gy")
+    right, left = lax.rem(me + 1, count), lax.rem(me + count - 1, count)
+    return (right // minor, lax.rem(right, minor)), (left // minor, lax.rem(left, minor))
+
+
+def greet(right, left):
+    barrier = pltpu.get_barrier_semaphore()
+    for neighbour in (left, right):
+        pl.semaphore_signal(barrier, inc=1, device_id=neighbour, device_id_type=MESH)
+
+
+def send_to(source, target, sems, index, device):
+    copy = pltpu.make_async_remote_copy(
+        src_ref=source,
+        dst_ref=target,
+        send_sem=sems.at[0, index],
+        recv_sem=sems.at[1, index],
+        device_id=device,
+        device_id_type=MESH,
+    )
+    copy.start()
+    return copy
+
+
+def front_kernel(
+    sizes, points_ref, send_ref, slot_ref, cot_ref, patch_ref, patch_cot_ref, outgoing, prev, next_, half, own, sems
+):
+    right, left = ring(sizes)
+    greet(right, left)
+    rows, cap = points_ref.shape[0], prev.shape[0]
+    shift = half.shape[0]
+    sender = as_column(send_ref[...])
+    outgoing[cap:, :] = mm(pick(sender[cap:], 0, rows), points_ref[...]).astype(BF16)
+    pl.semaphore_wait(pltpu.get_barrier_semaphore(), 2)
+    to_right = send_to(outgoing.at[pl.ds(cap, cap)], prev, sems, 0, right)
+    outgoing[:cap, :] = mm(pick(sender[:cap], 0, rows), points_ref[...]).astype(BF16)
+    to_left = send_to(outgoing.at[pl.ds(0, cap)], next_, sems, 1, left)
+    cot_copy = send_to(cot_ref.at[pl.ds(shift, shift)], patch_cot_ref.at[pl.ds(0, shift)], sems, 2, right)
+    patch_cot_ref[shift:, :] = cot_ref[:shift, :]
     column = as_column(slot_ref[...])
     for start in range(0, rows, CHUNK):
-        part = column[start : start + CHUNK]
-        total = mm(pick(part, 0, rows), points_ref[...])
-        total += mm(pick(part, rows, cap), prev_ref[...])
-        total += mm(pick(part, rows + cap, cap), next_ref[...])
-        out_ref[start : start + CHUNK, :] = total.astype(BF16)
-
-
-def back_kernel(grad_ref, slot_ref, out_ref):
-    out_ref[...] = mm(place(slot_ref[...], grad_ref.shape[0], out_ref.shape[0]), grad_ref[...]).astype(BF16)
-
-
-def final_kernel(grad_ref, slot_ref, send_ref, prev_ref, next_ref, out_ref):
-    rows, cap = grad_ref.shape[0], prev_ref.shape[0]
+        part = slice(start, start + CHUNK)
+        own[part, :] = mm(pick(column[part], 0, rows), points_ref[...])
+    to_right.wait_recv()
+    to_left.wait_recv()
+
+    def arrange(start):
+        part = slice(start, start + CHUNK)
+        total = own[part, :] + mm(pick(column[part], rows, cap), prev[...])
+        return (total + mm(pick(column[part], rows + cap, cap), next_[...])).astype(BF16)
+
+    for start in range(shift, rows, CHUNK):
+        half[start - shift : start - shift + CHUNK, :] = arrange(start)
+    half_copy = send_to(half, patch_ref.at[pl.ds(0, shift)], sems, 3, right)
+    for start in range(0, shift, CHUNK):
+        patch_ref[shift + start : shift + start + CHUNK, :] = arrange(start)
+    to_right.wait_send()
+    to_left.wait_send()
+    cot_copy.wait()
+    half_copy.wait()
+
+
+def back_kernel(
+    sizes, out_ref, grad_ref, slot_ref, send_ref, block_ref, points_ref, half, back, prev, next_, own, sems
+):
+    right, left = ring(sizes)
+    greet(right, left)
+    rows, cap = grad_ref.shape[0], prev.shape[0]
+    shift = half.shape[0]
+    pl.semaphore_wait(pltpu.get_barrier_semaphore(), 2)
+    grad_copy = send_to(grad_ref.at[pl.ds(0, shift)], half, sems, 0, left)
+    out_copy = send_to(out_ref.at[pl.ds(0, shift)], block_ref.at[pl.ds(shift, shift)], sems, 1, left)
+    block_ref[:shift, :] = out_ref[shift:, :]
+    first, second = slot_ref[:, :shift], slot_ref[:, shift:]
+    mine = grad_ref[shift:, :]
+    to_prev = mm(place(first, rows, cap), mine)
+    to_next = mm(place(first, rows + cap, cap), mine)
+    grad_copy.wait_recv()
+    theirs = half[...]
+    back[cap:, :] = (to_next + mm(place(second, rows + cap, cap), theirs)).astype(BF16)
+    to_right = send_to(back.at[pl.ds(cap, cap)], prev, sems, 2, right)
+    back[:cap, :] = (to_prev + mm(place(second, rows, cap), theirs)).astype(BF16)
+    to_left = send_to(back.at[pl.ds(0, cap)], next_, sems, 3, left)
     for start in range(0, rows, CHUNK):
-        total = mm(place(slot_ref[...], start, CHUNK), grad_ref[...])
-        total += mm(place(send_ref[:, :cap], start, CHUNK), prev_ref[...])
-        total += mm(place(send_ref[:, cap:], start, CHUNK), next_ref[...])
-        out_ref[start : start + CHUNK, :] = total.astype(BF16)
+        total = mm(place(first, start, CHUNK), mine)
+        own[start : start + CHUNK, :] = total + mm(place(second, start, CHUNK), theirs)
+    to_right.wait_recv()
+    to_left.wait_recv()
+    for start in range(0, rows, CHUNK):
+        total = own[start : start + CHUNK, :] + mm(place(send_ref[:, :cap], start, CHUNK), prev[...])
+        total += mm(place(send_ref[:, cap:], start, CHUNK), next_[...])
+        points_ref[start : start + CHUNK, :] = total.astype(BF16)
+    grad_copy.wait_send()
+    to_right.wait_send()
+    to_left.wait_send()
+    out_copy.wait()
 
 
 def block_kernel(
@@ -116,7 +190,7 @@
             recip[h, :, part] = inverse
         return carry
 
-    lax.fori_loop(0, H, forward_head, 0)
+    lax.fori_loop(0, H, forward_head, 0, unroll=2)
 
     for start in starts:
         part = slice(start, start + CHUNK)
@@ -158,7 +232,7 @@
         dqkv[2 * H + h] = grad_v.astype(BF16)
         return carry
 
-    lax.fori_loop(0, H, backward_head, 0)
+    lax.fori_loop(0, H, backward_head, 0, unroll=2)
 
     for start in starts:
         part = slice(start, start + CHUNK)
@@ -168,41 +242,44 @@
         grad_ref[part, :] = (gmixed[part, :] + normalize_back(unit, inv, grad_normed)).astype(BF16)
 
 
-def call(kernel, outs, args, scratch=(), vmem=32):
+def call(kernel, outs, args, scratch, vmem, collective=None):
     return pl.pallas_call(
         kernel,
         out_shape=outs,
         in_specs=[VMEM] * len(args),
         out_specs=jax.tree.map(lambda leaf: VMEM, outs),
         scratch_shapes=list(scratch),
-        compiler_params=pltpu.CompilerParams(vmem_limit_bytes=vmem * 2**20),
+        compiler_params=pltpu.CompilerParams(
+            vmem_limit_bytes=vmem * 2**20, collective_id=collective, has_side_effects=collective is not None
+        ),
     )(*args)
 
 
-def shards(points, send_rows, recv_slot, gain1, wqkv, proj, gain2, fc1, fc2, cotangent):
+def shards(sizes, points, send_rows, recv_slot, gain1, wqkv, proj, gain2, fc1, fc2, cotangent):
     rows, width = points.shape[1:]
     cap = send_rows.shape[2] // 2
     hd = proj.shape[0]
     head = hd // H
-    count = lax.axis_size(AXES)
-    up = [(i, (i + 1) % count) for i in range(count)]
-    down = [((i + 1) % count, i) for i in range(count)]
-    local, send, slot, cot = points[0], send_rows[0], recv_slot, cotangent[0]
-
-    def like(*shape):
-        return jax.ShapeDtypeStruct(shape, BF16)
-
-    cot_half = lax.ppermute(cot[SHIFT:], AXES, up)
-    outgoing = call(outgoing_kernel, like(2 * cap, width), (local, send))
-    from_prev = lax.ppermute(outgoing[cap:], AXES, up)
-    from_next = lax.ppermute(outgoing[:cap], AXES, down)
-    ordered = call(order_kernel, like(rows, width), (local, from_prev, from_next, slot))
-    half = lax.ppermute(ordered[SHIFT:], AXES, up)
-    patch = jnp.concatenate([half, ordered[:SHIFT]], axis=0)
-    patch_cot = jnp.concatenate([cot_half, cot[:SHIFT]], axis=0)
+    whole = jax.ShapeDtypeStruct((rows, width), BF16)
+    send = send_rows[0]
+    slots = pltpu.VMEM((cap, width), BF16)
+    half = pltpu.VMEM((SHIFT, width), BF16)
+    exchange = (
+        pltpu.VMEM((2 * cap, width), BF16), slots, slots, half,
+        pltpu.VMEM((rows, width), F32),
+        pltpu.SemaphoreType.DMA((2, 4)),
+    )
+    patch, patch_cot = call(
+        functools.partial(front_kernel, sizes),
+        (whole, whole),
+        (points[0], send, recv_slot, cotangent[0]),
+        exchange,
+        16,
+        0,
+    )
     patch_out, patch_grad = call(
         block_kernel,
-        (like(rows, width), like(rows, width)),
+        (whole, whole),
         (patch, patch_cot, gain1[None], wqkv, proj, gain2[None], fc1, fc2),
         (
             pltpu.VMEM((H, rows, rows), BF16),
@@ -215,18 +292,24 @@
             pltpu.VMEM((rows, width), F32),
             pltpu.VMEM((3 * H, head, rows), BF16),
         ),
-        vmem=60,
-    )
-    block_out = jnp.concatenate([patch_out[SHIFT:], lax.ppermute(patch_out[:SHIFT], AXES, down)], axis=0)
-    grad = jnp.concatenate([patch_grad[SHIFT:], lax.ppermute(patch_grad[:SHIFT], AXES, down)], axis=0)
-    back = call(back_kernel, like(2 * cap, width), (grad, slot))
-    back_prev = lax.ppermute(back[cap:], AXES, up)
-    back_next = lax.ppermute(back[:cap], AXES, down)
-    grad_points = call(final_kernel, like(rows, width), (grad, slot, send, back_prev, back_next))
+        60,
+    )
+    buffers, prev, next_, half, own, sems = exchange
+    block_out, grad_points = call(
+        functools.partial(back_kernel, sizes),
+        (whole, whole),
+        (patch_out, patch_grad, recv_slot, send),
+        (half, buffers, prev, next_, own, sems),
+        16,
+        1,
+    )
     return block_out[None], grad_points[None]
 
 
 def solution(mesh):
     split = P(None, AXES, None)
     in_specs = (split, split, P(None, AXES), P(), P(), P(), P(), P(), P(), split)
-    return jax.shard_map(shards, mesh=mesh, in_specs=in_specs, out_specs=(split, split), check_vma=False)
+    sizes = (mesh.shape["gx"], mesh.shape["gy"])
+    return jax.shard_map(
+        functools.partial(shards, sizes), mesh=mesh, in_specs=in_specs, out_specs=(split, split), check_vma=False
+    )

time: 119 us -> 104 us (0.87)
  waiting for transfers between devices: 28.7 us -> 0 us
  Pallas kernels: 71.1 us -> 94.9 us
  starting transfers between devices: 12.5 us -> 0 us
  local copies, waits for them, and re-layouts: 3.02 us -> 8.02 us
  other arithmetic: 2.52 us -> 0 us
    ppermute x8 -> x0, waiting for transfers between devices: 28.7 us -> none  [the longest x1 7.51 us: shards(): half = lax.ppermute(ordered[SHIFT:], AXES, up)]
    pallas_call x5 -> x3, Pallas kernels: 71.1 us -> 94.9 us  [call(): pl.pallas_call(kernel, out_shape=outs, in_specs=[VMEM] * len(args), out_s...]
    ppermute x8 -> x0, starting transfers between devices: 12.5 us -> none  [the longest x1 6.42 us: shards(): from_next = lax.ppermute(outgoing[:cap], AXES, down)]
    unnamed x10 -> x18, local copies, waits for them, and re-layouts: 1.74 us -> 8.02 us
    concatenate x3 -> x0, other arithmetic: 1.69 us -> none  [the longest x1 0.83 us: shards(): patch_cot = jnp.concatenate([cot_half, cot[:SHIFT]], axis=0)]
    slice x6 -> x0, local copies, waits for them, and re-layouts: 1.28 us -> none  [the longest x1 1.12 us: shards(): patch_grad[SHIFT:]]
  transfers between devices with their start and end apart: 8 -> 0, of which waited for: 7 -> 0; matrix products, arithmetic and copies ran while one was open for 2% -> 0% of each run, Pallas kernels for 2% -> 0%
where the time goes in v2:
time: 104 us
  Pallas kernels  94.9 us (91%)
  local copies, waits for them, and re-layouts  8.02 us (8%)
    pallas_call x3, Pallas kernels, call(): pl.pallas_call(kernel, out_shape=outs, in_specs=[VMEM] * len(args), out_s...  94.9 us
    unnamed x18, local copies, waits for them, and re-layouts  8.02 us

profile of v2, /device:TPU:0, one launch (start us, length us, event | category | flops | bytes accessed | tf_op | source)
XLA Modules:
  0.0 103.6 jit_solution(14257840944662777255)
XLA Ops:
  0.6 0.0 copy-start.6
  0.6 0.0 copy-start.7
  0.7 0.7 copy-done.6
  1.3 0.0 copy-done.7
  1.3 0.0 copy-start
  1.3 1.0 %copy-done = bf16[1,1024,256]{2,1,0:T(8,128)(2,1)S(1)} copy-done((bf16[1,1024,256]{2,1,0:T(8,128)(2,1)S(1)}, bf16[1,1024,256]{2,1,0:T(8,128)(2,1)}, u32[]{:S(2)}) %copy-start) | copy-done | bytes 524312
  2.4 0.0 copy-start.1
  2.4 1.0 %copy-done.1 = bf16[1,1024,256]{2,1,0:T(8,128)(2,1)S(1)} copy-done((bf16[1,1024,256]{2,1,0:T(8,128)(2,1)S(1)}, bf16[1,1024,256]{2,1,0:T(8,128)(2,1)}, u32[]{:S(2)}) %copy-start.1) | copy-done | bytes 524312
  3.4 20.3 %shard_map.113 = (bf16[1024,256]{1,0:T(8,128)(2,1)S(1)}, bf16[1024,256]{1,0:T(8,128)(2,1)S(1)}) custom-call(bf16[1024,256]{1,0:T(8,128)(2,1)S(1)} %bitcast.7, s32[1,768]{1,0:T(1,128)S(1)} %bitcast.11, s32[1,1024]{1,0:T(1,128)S(1)} %copy-done.6, bf16[1024,256]{1,0:T(8,128)(2,1)S(1)} %bitcast.8), custom_call_target="tpu_custom_call" | custom-call | tf_op jit(solution)/shard_map/pallas_call | solution.py:246
  23.7 0.0 copy-start.4
  23.8 0.8 copy-done.4
  24.5 0.0 copy-start.5
  24.5 0.8 copy-done.5
  25.3 60.3 %shard_map.114 = (bf16[1024,256]{1,0:T(8,128)(2,1)}, bf16[1024,256]{1,0:T(8,128)(2,1)}) custom-call(bf16[1024,256]{1,0:T(8,128)(2,1)} %copy-done.4, bf16[1024,256]{1,0:T(8,128)(2,1)} %copy-done.5, f32[1,256]{1,0:T(1,128)} %bitcast.13, bf16[256,768]{1,0:T(8,128)(2,1)} %wqkv_ref.1, bf16[256,256]{1,0:T(8,128)(2,1)} %proj_ref.1, f32[1,256]{1,0:T(1,128)} %bitcast.14, ...), custom_call_target="tpu_custom_call" | custom-call | tf_op jit(solution)/shard_map/pallas_call | solution.py:246
  85.7 0.0 copy-start.2
  85.7 1.0 %copy-done.2 = bf16[1024,256]{1,0:T(8,128)(2,1)S(1)} copy-done((bf16[1024,256]{1,0:T(8,128)(2,1)S(1)}, bf16[1024,256]{1,0:T(8,128)(2,1)}, u32[]{:S(2)}) %copy-start.2) | copy-done | bytes 524312
  86.7 0.0 copy-start.3
  86.7 1.0 %copy-done.3 = bf16[1024,256]{1,0:T(8,128)(2,1)S(1)} copy-done((bf16[1024,256]{1,0:T(8,128)(2,1)S(1)}, bf16[1024,256]{1,0:T(8,128)(2,1)}, u32[]{:S(2)}) %copy-start.3) | copy-done | bytes 524312
  87.8 14.2 %shard_map.115 = (bf16[1024,256]{1,0:T(8,128)(2,1)S(1)}, bf16[1024,256]{1,0:T(8,128)(2,1)S(1)}) custom-call(bf16[1024,256]{1,0:T(8,128)(2,1)S(1)} %copy-done.2, bf16[1024,256]{1,0:T(8,128)(2,1)S(1)} %copy-done.3, s32[1,1024]{1,0:T(1,128)S(1)} %copy-done.6, s32[1,768]{1,0:T(1,128)S(1)} %bitcast.12), custom_call_target="tpu_custom_call" | custom-call | tf_op jit(solution)/shard_map/pallas_call | solution.py:246
  102.0 0.8 copy.14
  102.8 0.8 copy.15
Async XLA Ops:
  0.6 0.7 copy-start.6
  0.6 0.7 copy-start.7
  1.3 1.0 %copy-start = (bf16[1,1024,256]{2,1,0:T(8,128)(2,1)S(1)}, bf16[1,1024,256]{2,1,0:T(8,128)(2,1)}, u32[]{:S(2)}) copy-start(bf16[1,1024,256]{2,1,0:T(8,128)(2,1)} %param.10) | copy-start | bytes 1572868
  2.4 1.0 %copy-start.1 = (bf16[1,1024,256]{2,1,0:T(8,128)(2,1)S(1)}, bf16[1,1024,256]{2,1,0:T(8,128)(2,1)}, u32[]{:S(2)}) copy-start(bf16[1,1024,256]{2,1,0:T(8,128)(2,1)} %param.19) | copy-start | bytes 1572868
  23.7 0.8 copy-start.4
  24.5 0.8 copy-start.5
  85.7 1.0 %copy-start.2 = (bf16[1024,256]{1,0:T(8,128)(2,1)S(1)}, bf16[1024,256]{1,0:T(8,128)(2,1)}, u32[]{:S(2)}) copy-start(bf16[1024,256]{1,0:T(8,128)(2,1)} %get-tuple-element.10.out_ref) | copy-start | bytes 1572868
  86.7 1.0 %copy-start.3 = (bf16[1024,256]{1,0:T(8,128)(2,1)S(1)}, bf16[1024,256]{1,0:T(8,128)(2,1)}, u32[]{:S(2)}) copy-start(bf16[1024,256]{1,0:T(8,128)(2,1)} %get-tuple-element.11.grad_ref) | copy-start | bytes 1572868

commit v3 on v2

--- a/solution.py
+++ b/solution.py
@@ -178,13 +178,13 @@
 
     def forward_head(h, carry):
         q_rows = q3[h].T
-        v_rows = v3[h].T
+        values = v3[h]
         keys = k3[h]
         for start in starts:
             part = slice(start, start + CHUNK)
             weights = jnp.exp(mm(q_rows[part], keys)).astype(BF16)
             exps[h, part, :] = weights
-            summed = mm(weights, v_rows).T
+            summed = mm_t(values, weights)
             inverse = 1.0 / summed[head : head + 1]
             attn[h, :, part] = summed[:head] * inverse
             recip[h, :, part] = inverse
@@ -217,7 +217,7 @@
 
     def backward_head(h, carry):
         g_rows = gext[h].T
-        k_rows = k3[h].T
+        keys = k3[h]
         values = v3[h]
         grad_k = jnp.zeros((head, rows), F32)
         grad_v = jnp.zeros((head, rows), F32)
@@ -227,7 +227,7 @@
             scores = (weights.astype(F32) * mm(g_rows[part], values)).astype(BF16)
             grad_v += mm(gext[h, :head, part], weights)
             grad_k += mm(q3[h, :, part], scores)
-            dqkv[h, :, part] = (mm(scores, k_rows).T * scale).astype(BF16)
+            dqkv[h, :, part] = (mm_t(keys, scores) * scale).astype(BF16)
         dqkv[H + h] = grad_k.astype(BF16)
         dqkv[2 * H + h] = grad_v.astype(BF16)
         return carry
@@ -274,7 +274,7 @@
         (whole, whole),
         (points[0], send, recv_slot, cotangent[0]),
         exchange,
-        16,
+        60,
         0,
     )
     patch_out, patch_grad = call(
@@ -300,7 +300,7 @@
         (whole, whole),
         (patch_out, patch_grad, recv_slot, send),
         (half, buffers, prev, next_, own, sems),
-        16,
+        60,
         1,
     )
     return block_out[None], grad_points[None]

time: 104 us -> 103 us (level)
  local copies, waits for them, and re-layouts: 8.02 us -> 2.72 us
  Pallas kernels: 94.9 us -> 99.1 us
    unnamed x18 -> x4, local copies, waits for them, and re-layouts: 8.02 us -> 2.72 us
    pallas_call x3, Pallas kernels: 94.9 us -> 99.1 us  [call(): pl.pallas_call(kernel, out_shape=outs, in_specs=[VMEM] * len(args), out_s...]
where the time goes in v3:
time: 103 us; the launch traced here: 102 us
  Pallas kernels  99.1 us (96%)
  local copies, waits for them, and re-layouts  2.72 us (3%)
    pallas_call x3, Pallas kernels, call(): pl.pallas_call(kernel, out_shape=outs, in_specs=[VMEM] * len(args), out_s...  99.1 us
    unnamed x4, local copies, waits for them, and re-layouts  2.72 us

profile of v3, /device:TPU:0, one launch (start us, length us, event | category | flops | bytes accessed | tf_op | source)
XLA Modules:
  0.0 102.5 jit_solution(6402025285817744912)
XLA Ops:
  0.6 22.5 %shard_map.113 = (bf16[1024,256]{1,0:T(8,128)(2,1)}, bf16[1024,256]{1,0:T(8,128)(2,1)}) custom-call(bf16[1024,256]{1,0:T(8,128)(2,1)} %bitcast.7, s32[1,768]{1,0:T(1,128)} %bitcast.11, s32[1,1024]{1,0:T(1,128)} %slot_ref.3, bf16[1024,256]{1,0:T(8,128)(2,1)} %bitcast.8), custom_call_target="tpu_custom_call" | custom-call | tf_op jit(solution)/shard_map/pallas_call | solution.py:246
  23.2 60.2 %shard_map.114 = (bf16[1024,256]{1,0:T(8,128)(2,1)}, bf16[1024,256]{1,0:T(8,128)(2,1)}) custom-call(bf16[1024,256]{1,0:T(8,128)(2,1)} %get-tuple-element.8.x_ref, bf16[1024,256]{1,0:T(8,128)(2,1)} %get-tuple-element.9.cot_ref, f32[1,256]{1,0:T(1,128)} %bitcast.13, bf16[256,768]{1,0:T(8,128)(2,1)} %wqkv_ref.1, bf16[256,256]{1,0:T(8,128)(2,1)} %proj_ref.1, ...), custom_call_target="tpu_custom_call" | custom-call | tf_op jit(solution)/shard_map/pallas_call | solution.py:246
  83.3 16.4 %shard_map.115 = (bf16[1024,256]{1,0:T(8,128)(2,1)}, bf16[1024,256]{1,0:T(8,128)(2,1)}) custom-call(bf16[1024,256]{1,0:T(8,128)(2,1)} %get-tuple-element.10.out_ref, bf16[1024,256]{1,0:T(8,128)(2,1)} %get-tuple-element.11.grad_ref, s32[1,1024]{1,0:T(1,128)} %slot_ref.3, s32[1,768]{1,0:T(1,128)} %bitcast.12), custom_call_target="tpu_custom_call" | custom-call | tf_op jit(solution)/shard_map/pallas_call | solution.py:246
  99.7 0.0 copy-start
  99.7 1.9 %copy.14 = bf16[1,1024,256]{2,1,0:T(8,128)(2,1)} copy(bf16[1,1024,256]{2,1,0:T(8,128)(2,1)} %bitcast.10) | data formatting | bytes 1048576
  101.7 0.0 copy-done
  101.7 0.8 copy.15
Async XLA Ops:
  99.7 1.9 %copy-start = (bf16[1024,256]{1,0:T(8,128)(2,1)S(1)}, bf16[1024,256]{1,0:T(8,128)(2,1)}, u32[]{:S(2)}) copy-start(bf16[1024,256]{1,0:T(8,128)(2,1)} %get-tuple-element.13) | copy-start | bytes 1572868

commit v4 on v3

v4 whole, which is shorter than its diff:
```python
import functools
import math

import jax
import jax.numpy as jnp
from jax import lax
from jax.experimental import pallas as pl
from jax.experimental.pallas import tpu as pltpu
from jax.sharding import PartitionSpec as P

H = 16
SHIFT = 512
CHUNK = 256
EPS = 1e-05
AXES = ("gx", "gy")
F32 = jnp.float32
BF16 = jnp.bfloat16
VMEM = pl.BlockSpec(memory_space=pltpu.VMEM)
MESH = pl.DeviceIdType.MESH


def mm(a, b):
    return lax.dot_general(a, b, (((1,), (0,)), ((), ())), preferred_element_type=F32)


def mm_t(a, b):
    return lax.dot_general(a, b, (((1,), (1,)), ((), ())), preferred_element_type=F32)


def normalize(rows):
    centered = rows - jnp.mean(rows, axis=-1, keepdims=True)
    inv = lax.rsqrt(jnp.mean(centered * centered, axis=-1, keepdims=True) + EPS)
    return centered * inv, inv


def normalize_back(unit, inv, grad):
    inner = jnp.mean(grad * unit, axis=-1, keepdims=True)
    return inv * (grad - jnp.mean(grad, axis=-1, keepdims=True) - unit * inner)


def as_column(row):
    wide = jnp.broadcast_to(row.astype(F32), (8, row.shape[1]))
    return wide.T[:, :1].astype(jnp.int32)


def pick(column, first, count):
    ids = lax.broadcasted_iota(jnp.int32, (column.shape[0], count), 1) + first
    return (column == ids).astype(F32).astype(BF16)


def place(row, first, count):
    ids = lax.broadcasted_iota(jnp.int32, (count, row.shape[1]), 0) + first
    return (row == ids).astype(F32).astype(BF16)


def ring(sizes):
    major, minor = sizes
    count = major * minor
    me = lax.axis_index("gx") * minor + lax.axis_index("gy")
    right, left = lax.rem(me + 1, count), lax.rem(me + count - 1, count)
    return (right // minor, lax.rem(right, minor)), (left // minor, lax.rem(left, minor))


def greet(right, left):
    barrier = pltpu.get_barrier_semaphore()
    for neighbour in (left, right):
        pl.semaphore_signal(barrier, inc=1, device_id=neighbour, device_id_type=MESH)


def send_to(source, target, sems, index, device):
    copy = pltpu.make_async_remote_copy(
        src_ref=source,
        dst_ref=target,
        send_sem=sems.at[0, index],
        recv_sem=sems.at[1, index],
        device_id=device,
        device_id_type=MESH,
    )
    copy.start()
    return copy


def whole_kernel(
    sizes,
    points_ref, send_ref, slot_ref, cot_ref, gain1_ref, wqkv_ref, proj_ref, gain2_ref, fc1_ref, fc2_ref,
    block_ref, points_grad_ref,
    outgoing, prev, next_, half, own, x_ref, cot_half, leaving_out, leaving_grad, grad_half, mine_ref,
    back, back_prev, back_next,
    exps, q3, k3, v3, attn, recip, gext, gmixed, dqkv, sems,
):
    right, left = ring(sizes)
    greet(right, left)
    rows, cap = points_ref.shape[0], prev.shape[0]
    shift = half.shape[0]
    hd = proj_ref.shape[0]
    head = hd // H
    scale = 1.0 / math.sqrt(head)
    starts = range(0, rows, CHUNK)

    sender = as_column(send_ref[...])
    outgoing[cap:, :] = mm(pick(sender[cap:], 0, rows), points_ref[...]).astype(BF16)
    pl.semaphore_wait(pltpu.get_barrier_semaphore(), 2)
    to_right = send_to(outgoing.at[pl.ds(cap, cap)], prev, sems, 0, right)
    outgoing[:cap, :] = mm(pick(sender[:cap], 0, rows), points_ref[...]).astype(BF16)
    to_left = send_to(outgoing.at[pl.ds(0, cap)], next_, sems, 1, left)
    column = as_column(slot_ref[...])
    for start in starts:
        part = slice(start, start + CHUNK)
        own[part, :] = mm(pick(column[part], 0, rows), points_ref[...])
    wqkv_t = wqkv_ref[...].T
    tail = lax.broadcasted_iota(jnp.int32, (H, head, rows), 1)
    v3[:, head:, :] = jnp.where(tail < 2, 1.0, 0.0).astype(BF16)

    to_right.wait_recv()
    to_left.wait_recv()

    def arrange(start):
        part = slice(start, start + CHUNK)
        total = own[part, :] + mm(pick(column[part], rows, cap), prev[...])
        return (total + mm(pick(column[part], rows + cap, cap), next_[...])).astype(BF16)

    for start in range(shift, rows, CHUNK):
        half[start - shift : start - shift + CHUNK, :] = arrange(start)
    half_copy = send_to(half, x_ref.at[pl.ds(0, shift)], sems, 3, right)
    cot_copy = send_to(cot_ref.at[pl.ds(shift, shift)], cot_half, sems, 2, right)

    def project(start):
        part = slice(start, start + CHUNK)
        unit, inv = normalize(x_ref[part, :].astype(F32))
        qkv = mm_t(wqkv_t, (unit * gain1_ref[...]).astype(BF16)).astype(BF16)
        q3[:, :, part] = (qkv[:hd].astype(F32) * scale).astype(BF16).reshape(H, head, CHUNK)
        k3[:, :, part] = qkv[hd : 2 * hd].reshape(H, head, CHUNK)
        v3[:, :head, part] = qkv[2 * hd :].reshape(H, head, CHUNK)

    for start in range(0, shift, CHUNK):
        x_ref[shift + start : shift + start + CHUNK, :] = arrange(start)
    for start in range(shift, rows, CHUNK):
        project(start)
    half_copy.wait_recv()
    for start in range(0, shift, CHUNK):
        project(start)

    def forward_head(h, carry):
        q_rows = q3[h].T
        values = v3[h]
        keys = k3[h]
        for start in starts:
            part = slice(start, start + CHUNK)
            weights = jnp.exp(mm(q_rows[part], keys)).astype(BF16)
            exps[h, part, :] = weights
            summed = mm_t(values, weights)
            inverse = 1.0 / summed[head : head + 1]
            attn[h, :, part] = summed[:head] * inverse
            recip[h, :, part] = inverse
        return carry

    lax.fori_loop(0, H, forward_head, 0, unroll=2)

    cot_copy.wait_recv()
    for start in starts:
        part = slice(start, start + CHUNK)
        attn_t = attn[:, :, part].reshape(hd, CHUNK)
        mixed = x_ref[part, :].astype(F32) + mm(attn_t.T.astype(BF16), proj_ref[...])
        unit, inv = normalize(mixed)
        pre = mm((unit * gain2_ref[...]).astype(BF16), fc1_ref[...])
        cdf = 0.5 + 0.5 * lax.erf(pre * math.sqrt(0.5))
        block_out = (mixed + mm((pre * cdf).astype(BF16), fc2_ref[...])).astype(BF16)
        slope = cdf + pre * (math.sqrt(0.5 / math.pi) * jnp.exp(-0.5 * pre * pre))
        if start < shift:
            leaving_out[part, :] = block_out
            cot = cot_half[part, :]
        else:
            block_ref[start - shift : start - shift + CHUNK, :] = block_out
            cot = cot_ref[start - shift : start - shift + CHUNK, :]
        grad_pre = (mm_t(cot, fc2_ref[...]) * slope).astype(BF16)
        grad_normed = mm_t(grad_pre, fc1_ref[...]) * gain2_ref[...]
        grad_mixed = cot.astype(F32) + normalize_back(unit, inv, grad_normed)
        gmixed[part, :] = grad_mixed
        grad_attn = mm_t(proj_ref[...], grad_mixed.astype(BF16)).astype(BF16).astype(F32)
        inverse = recip[:, :, part]
        inner = jnp.sum((grad_attn * attn_t).reshape(H, head, CHUNK), axis=1, keepdims=True) * inverse
        inner_hi = inner.astype(BF16).astype(F32)
        gext[:, :head, part] = (grad_attn.reshape(H, head, CHUNK) * inverse).astype(BF16)
        which = lax.broadcasted_iota(jnp.int32, (H, head, CHUNK), 1)
        rest = jnp.where(which == 0, -inner_hi, jnp.where(which == 1, inner_hi - inner, 0.0))
        gext[:, head:, part] = rest.astype(BF16)
    out_copy = send_to(leaving_out, block_ref.at[pl.ds(shift, shift)], sems, 4, left)

    def backward_head(h, carry):
        g_rows = gext[h].T
        keys = k3[h]
        values = v3[h]
        grad_k = jnp.zeros((head, rows), F32)
        grad_v = jnp.zeros((head, rows), F32)
        for start in starts:
            part = slice(start, start + CHUNK)
            weights = exps[h, part, :]
            scores = (weights.astype(F32) * mm(g_rows[part], values)).astype(BF16)
            grad_v += mm(gext[h, :head, part], weights)
            grad_k += mm(q3[h, :, part], scores)
            dqkv[h, :, part] = (mm_t(keys, scores) * scale).astype(BF16)
        dqkv[H + h] = grad_k.astype(BF16)
        dqkv[2 * H + h] = grad_v.astype(BF16)
        return carry

    lax.fori_loop(0, H, backward_head, 0, unroll=2)

    def input_grad(start):
        part = slice(start, start + CHUNK)
        grad_qkv = dqkv[:, :, part].reshape(3 * hd, CHUNK).astype(F32).T.astype(BF16)
        grad_normed = mm_t(grad_qkv, wqkv_ref[...]) * gain1_ref[...]
        unit, inv = normalize(x_ref[part, :].astype(F32))
        return (gmixed[part, :] + normalize_back(unit, inv, grad_normed)).astype(BF16)

    for start in range(0, shift, CHUNK):
        leaving_grad[start : start + CHUNK, :] = input_grad(start)
    grad_copy = send_to(leaving_grad, grad_half, sems, 5, left)
    for start in range(shift, rows, CHUNK):
        mine_ref[start - shift : start - shift + CHUNK, :] = input_grad(start)

    first, second = slot_ref[:, :shift], slot_ref[:, shift:]
    mine = mine_ref[...]
    own[: 2 * cap, :] = mm(place(first, rows, 2 * cap), mine)
    grad_copy.wait_recv()
    theirs = grad_half[...]
    to_next = mm(place(second, rows + cap, cap), theirs)
    back[cap:, :] = (own[cap : 2 * cap, :] + to_next).astype(BF16)
    back_right = send_to(back.at[pl.ds(cap, cap)], back_prev, sems, 6, right)
    to_prev = mm(place(second, rows, cap), theirs)
    back[:cap, :] = (own[:cap, :] + to_prev).astype(BF16)
    back_left = send_to(back.at[pl.ds(0, cap)], back_next, sems, 7, left)
    for start in starts:
        total = mm(place(first, start, CHUNK), mine)
        own[start : start + CHUNK, :] = total + mm(place(second, start, CHUNK), theirs)
    to_right.wait_send()
    to_left.wait_send()
    half_copy.wait_send()
    cot_copy.wait_send()
    out_copy.wait()
    grad_copy.wait_send()
    back_right.wait_recv()
    back_left.wait_recv()
    for start in starts:
        total = own[start : start + CHUNK, :] + mm(place(send_ref[:, :cap], start, CHUNK), back_prev[...])
        total += mm(place(send_ref[:, cap:], start, CHUNK), back_next[...])
        points_grad_ref[start : start + CHUNK, :] = total.astype(BF16)
    back_right.wait_send()
    back_left.wait_send()


def shards(sizes, points, send_rows, recv_slot, gain1, wqkv, proj, gain2, fc1, fc2, cotangent):
    rows, width = points.shape[1:]
    cap = send_rows.shape[2] // 2
    hd = proj.shape[0]
    head = hd // H
    whole = jax.ShapeDtypeStruct((rows, width), BF16)
    args = (points[0], send_rows[0], recv_slot, cotangent[0], gain1[None], wqkv, proj, gain2[None], fc1, fc2)
    both = pltpu.VMEM((2 * cap, width), BF16)
    slots = pltpu.VMEM((cap, width), BF16)
    half = pltpu.VMEM((SHIFT, width), BF16)
    block_out, grad_points = pl.pallas_call(
        functools.partial(whole_kernel, sizes),
        out_shape=(whole, whole),
        in_specs=[VMEM] * len(args),
        out_specs=(VMEM, VMEM),
        scratch_shapes=[
            both, slots, slots, half,
            pltpu.VMEM((rows, width), F32),
            pltpu.VMEM((rows, width), BF16),
            half, half, half, half, half,
            both, slots, slots,
            pltpu.VMEM((H, rows, rows), BF16),
            pltpu.VMEM((H, head, rows), BF16),
            pltpu.VMEM((H, head, rows), BF16),
            pltpu.VMEM((H, 2 * head, rows), BF16),
            pltpu.VMEM((H, head, rows), F32),
            pltpu.VMEM((H, 1, rows), F32),
            pltpu.VMEM((H, 2 * head, rows), BF16),
            pltpu.VMEM((rows, width), F32),
            pltpu.VMEM((3 * H, head, rows), BF16),
            pltpu.SemaphoreType.DMA((2, 8)),
        ],
        compiler_params=pltpu.CompilerParams(
            vmem_limit_bytes=60 * 2**20, collective_id=0, has_side_effects=True
        ),
    )(*args)
    return block_out[None], grad_points[None]


def solution(mesh):
    split = P(None, AXES, None)
    in_specs = (split, split, P(None, AXES), P(), P(), P(), P(), P(), P(), split)
    sizes = (mesh.shape["gx"], mesh.shape["gy"])
    return jax.shard_map(
        functools.partial(shards, sizes), mesh=mesh, in_specs=in_specs, out_specs=(split, split), check_vma=False
    )
```

time: 103 us -> 97.1 us (0.943)
  Pallas kernels: 99.1 us -> 93.5 us
    pallas_call x3 -> x1, Pallas kernels: 99.1 us -> 93.5 us  [shards(): pl.pallas_call(functools.partial(whole_kernel, sizes), out_shape=(whole,...]
where the time goes in v4:
time: 97.1 us; the launch traced here: 96.9 us
  Pallas kernels  93.5 us (96%)
  local copies, waits for them, and re-layouts  2.72 us (3%)
    pallas_call x1, Pallas kernels, shards(): pl.pallas_call(functools.partial(whole_kernel, sizes), out_shape=(whole,...  93.5 us
    unnamed x4, local copies, waits for them, and re-layouts  2.72 us

profile of v4, /device:TPU:0, one launch (start us, length us, event | category | flops | bytes accessed | tf_op | source)
XLA Modules:
  0.0 96.9 jit_solution(4475151696085906871)
XLA Ops:
  0.6 93.5 %shard_map.113 = (bf16[1024,256]{1,0:T(8,128)(2,1)}, bf16[1024,256]{1,0:T(8,128)(2,1)}) custom-call(bf16[1024,256]{1,0:T(8,128)(2,1)} %bitcast.7, s32[1,768]{1,0:T(1,128)} %bitcast.11, s32[1,1024]{1,0:T(1,128)} %slot_ref.1, bf16[1024,256]{1,0:T(8,128)(2,1)} %bitcast.8, f32[1,256]{1,0:T(1,128)} %bitcast.12, bf16[256,768]{1,0:T(8,128)(2,1)} %wqkv_ref.1, ...), custom_call_target="tpu_custom_call" | custom-call | tf_op jit(solution)/shard_map/pallas_call | solution.py:261
  94.2 0.0 copy-start
  94.2 1.9 %copy.14 = bf16[1,1024,256]{2,1,0:T(8,128)(2,1)} copy(bf16[1,1024,256]{2,1,0:T(8,128)(2,1)} %bitcast.10) | data formatting | bytes 1048576
  96.1 0.0 copy-done
  96.1 0.8 copy.15
Async XLA Ops:
  94.2 1.9 %copy-start = (bf16[1024,256]{1,0:T(8,128)(2,1)S(1)}, bf16[1024,256]{1,0:T(8,128)(2,1)}, u32[]{:S(2)}) copy-start(bf16[1024,256]{1,0:T(8,128)(2,1)} %get-tuple-element.5) | copy-start | bytes 1572868

commit v5 on v4

--- a/solution.py
+++ b/solution.py
@@ -154,7 +154,7 @@
             recip[h, :, part] = inverse
         return carry
 
-    lax.fori_loop(0, H, forward_head, 0, unroll=2)
+    lax.fori_loop(0, H, forward_head, 0, unroll=4)
 
     cot_copy.wait_recv()
     for start in starts:
@@ -195,7 +195,7 @@
         for start in starts:
             part = slice(start, start + CHUNK)
             weights = exps[h, part, :]
-            scores = (weights.astype(F32) * mm(g_rows[part], values)).astype(BF16)
+            scores = weights * mm(g_rows[part], values).astype(BF16)
             grad_v += mm(gext[h, :head, part], weights)
             grad_k += mm(q3[h, :, part], scores)
             dqkv[h, :, part] = (mm_t(keys, scores) * scale).astype(BF16)
@@ -203,7 +203,7 @@
         dqkv[2 * H + h] = grad_v.astype(BF16)
         return carry
 
-    lax.fori_loop(0, H, backward_head, 0, unroll=2)
+    lax.fori_loop(0, H, backward_head, 0, unroll=4)
 
     def input_grad(start):
         part = slice(start, start + CHUNK)

time: 97.1 us -> 94 us (0.968)
  Pallas kernels: 93.5 us -> 90.5 us
    pallas_call x1, Pallas kernels: 93.5 us -> 90.5 us  [shards(): pl.pallas_call(functools.partial(whole_kernel, sizes), out_shape=(whole,...]
where the time goes in v5:
time: 94 us; the launch traced here: 93.8 us
  Pallas kernels  90.5 us (96%)
  local copies, waits for them, and re-layouts  2.72 us (3%)
    pallas_call x1, Pallas kernels, shards(): pl.pallas_call(functools.partial(whole_kernel, sizes), out_shape=(whole,...  90.5 us
    unnamed x4, local copies, waits for them, and re-layouts  2.72 us

profile of v5, /device:TPU:0, one launch (start us, length us, event | category | flops | bytes accessed | tf_op | source)
XLA Modules:
  0.0 93.8 jit_solution(6889684717221958569)
XLA Ops:
  0.6 90.5 %shard_map.113 = (bf16[1024,256]{1,0:T(8,128)(2,1)}, bf16[1024,256]{1,0:T(8,128)(2,1)}) custom-call(bf16[1024,256]{1,0:T(8,128)(2,1)} %bitcast.7, s32[1,768]{1,0:T(1,128)} %bitcast.11, s32[1,1024]{1,0:T(1,128)} %slot_ref.1, bf16[1024,256]{1,0:T(8,128)(2,1)} %bitcast.8, f32[1,256]{1,0:T(1,128)} %bitcast.12, bf16[256,768]{1,0:T(8,128)(2,1)} %wqkv_ref.1, ...), custom_call_target="tpu_custom_call" | custom-call | tf_op jit(solution)/shard_map/pallas_call | solution.py:261
  91.1 0.0 copy-start
  91.1 1.9 %copy.14 = bf16[1,1024,256]{2,1,0:T(8,128)(2,1)} copy(bf16[1,1024,256]{2,1,0:T(8,128)(2,1)} %bitcast.10) | data formatting | bytes 1048576
  93.0 0.0 copy-done
  93.1 0.8 copy.15
Async XLA Ops:
  91.1 1.9 %copy-start = (bf16[1024,256]{1,0:T(8,128)(2,1)S(1)}, bf16[1024,256]{1,0:T(8,128)(2,1)}, u32[]{:S(2)}) copy-start(bf16[1024,256]{1,0:T(8,128)(2,1)} %get-tuple-element.5) | copy-start | bytes 1572868
